TPU v7x, 256 devices: a whole 4x4x8 slice. The times are simulated.
256 devices in a mesh: ctx: 16 (over x, y_lo, core), exp: 16 (over z, y_hi).
Axes of the slice: x: 4, y: 4 (y_hi: 2, y_lo: 2; y = y_hi * 2 + y_lo), z: 8, core: 2. Of those that a mesh axis runs over, the one named last changes fastest.
Arguments:
- queries: bfloat16 [2048, 6144], P('ctx', 'exp'), may hold values from -8 to 8
- keys: bfloat16 [2048, 1024], P('ctx'), may hold values from -8 to 8
- values: bfloat16 [2048, 1024], P('ctx'), may hold values from -6 to 6
- segment_ids: int32 [2048], P('ctx'), may hold values from 0 to 1, never falling along the last dimension, each value on 1 to 1536 neighbouring positions
- residual: bfloat16 [2048, 6144], P(('ctx', 'exp')), may hold values from -6 to 6
- w_out: bfloat16 [6144, 6144], P('exp', 'ctx'), may hold values from -0.078125 to 0.078125
- norm_gain: float32 [6144], replicated, may hold values from 0.25 to 1.75
- w_router: bfloat16 [6144, 8], replicated, may hold values from -0.078125 to 0.078125
- routes: int32 [2048, 2], P(('ctx', 'exp')), may hold values from 0 to 7, all different within a row; in each aligned block of 8 rows (0 to 7, 8 to 15, ...) at most 3 rows name the same one
- w_gate: bfloat16 [16, 6144, 4096], P('exp', None, 'ctx'), may hold values from -0.078125 to 0.078125
- w_up: bfloat16 [16, 6144, 4096], P('exp', None, 'ctx'), may hold values from -0.078125 to 0.078125
- w_down: bfloat16 [16, 4096, 6144], P('exp', 'ctx'), may hold values from -0.0625 to 0.0625
Outputs:
- layer_out: bfloat16 [2048, 6144], P(('ctx', 'exp'))
Inputs may be any that keep to these rules, and one draw needn't show every extreme that they name: `routes`: in each aligned block of 8 tokens (one device's tokens) no expert is named more than 3 times; some block names one exactly 3 times. A token's two entries differ. `segment_ids`: never falling: the first 512 to 1536 positions are 0, the rest 1.
All inputs are finite; a program needn't handle non-finite values.
Results may differ from a plain program's by a relative error of at most 0.02.
Values may be sent and summed in bfloat16 or wider, within the bound.
No kernel may reach another device: no remote copies, remote signals or barrier semaphores. Data moves between devices by JAX's collectives and lax.ppermute only.
A program may use at most 128 MiB of HBM per device.

v0:
```python
import functools

import jax
import jax.numpy as jnp
import numpy as np
from jax import lax
from jax.experimental import pallas as pl
from jax.experimental.pallas import tpu as pltpu
from jax.sharding import Mesh, PartitionSpec as P

HEADS = 48
KVH = 8
HD = 128
EXPERTS = 8
NEG_FILL = -1e30
EPSILON = 1e-05
SLOTS = 3

CTX, EXP, PLANE = ("x", "yl", "core"), ("z", "yh"), ("x", "yl", "core", "yh")
BF, F32 = jnp.bfloat16, jnp.float32


def swap(value, axis):
    return lax.ppermute(value, axis, [(0, 1), (1, 0)])


def plane_shift(value, by, turn):
    def index(x, y, core):
        return ((x * 2 + y % 2) * 2 + core) * 2 + y // 2

    pairs = [
        (
            index(x, y, core),
            index((x + by) % 4, y, core) if core == turn else index(x, (y + by) % 4, core),
        )
        for x in range(4)
        for y in range(4)
        for core in (0, 1)
    ]
    return lax.ppermute(value, PLANE, pairs)


def total(first, *others):
    result = first.astype(F32)
    for other in others:
        result = result + other.astype(F32)
    return result


def attend(queries, keys, values, segment_ids):
    z = lax.axis_index("z")
    rows = queries.shape[0]
    seg_row = jnp.pad(segment_ids.astype(BF)[None, :], ((0, 7), (0, rows)))
    block = jnp.concatenate(
        [
            jnp.concatenate(
                [
                    lax.dynamic_slice_in_dim(keys, z * HD, HD, 1),
                    lax.dynamic_slice_in_dim(values, z * HD, HD, 1),
                ],
                axis=1,
            ),
            seg_row,
        ],
        axis=0,
    )
    x, yl, core = lax.axis_index("x"), lax.axis_index("yl"), lax.axis_index("core")
    along_x = [lax.ppermute(block, "x", [(i, (i + by) % 4) for i in range(4)]) for by in (1, 3, 2)]
    blocks = jnp.stack([block] + along_x)
    blocks = jnp.stack([blocks, swap(blocks, "yl")])
    blocks = jnp.stack([blocks, swap(blocks, "core")])
    places = [
        ((x + dx) & 3) * 4 + ((yl + dy) & 1) * 2 + ((core + dc) & 1)
        for dc in (0, 1)
        for dy in (0, 1)
        for dx in (0, 3, 1, 2)
    ]
    blocks = blocks.reshape(16, rows + 8, 2 * HD)
    key_rows = blocks[:, :rows, :HD].reshape(16 * rows, HD)
    value_rows = blocks[:, :rows, HD:].reshape(16 * rows, HD)
    seg_keys = blocks[:, rows, :rows].reshape(16 * rows).astype(jnp.int32)
    row_ids = jnp.arange(rows, dtype=jnp.int32)
    key_pos = (jnp.stack(places)[:, None] * rows + row_ids[None, :]).reshape(16 * rows)
    query_pos = (x * 4 + yl * 2 + core) * rows + row_ids
    allowed = (key_pos[None, :] <= query_pos[:, None]) & (
        seg_keys[None, :] == segment_ids[:, None]
    )
    head_count = queries.shape[1] // HD
    query_heads = queries.reshape(rows, head_count, HD)
    scores = jnp.einsum("qrd,kd->rqk", query_heads, key_rows, preferred_element_type=F32)
    scores = jnp.where(allowed[None], scores * HD ** (-0.5), NEG_FILL)
    peak = jnp.max(scores, axis=-1, keepdims=True)
    weights = jnp.where(allowed[None], jnp.exp(scores - peak), 0.0)
    sums = jnp.sum(weights, axis=-1)
    update = jnp.einsum(
        "rqk,kd->rqd", weights.astype(BF), value_rows, preferred_element_type=F32
    )
    attention = (update / sums[..., None]).astype(BF)
    return attention.transpose(1, 0, 2).reshape(rows, head_count * HD)


def gather_plane(rows):
    near = [plane_shift(rows, by, 0) for by in (1, -1, 2)]
    rows = jnp.concatenate([rows] + near)
    half = rows.shape[0] // 2
    left, right = plane_shift(rows, 1, 1), plane_shift(rows, -1, 1)
    far_first = plane_shift(left[:half], 1, 1)
    far_second = plane_shift(right[half:], -1, 1)
    mine = [rows, left, right, far_first, far_second]
    return mine, [swap(block, "core") for block in mine]


def scatter_plane(mine, other):
    far_first, far_second = [total(mine[i], swap(other[i], "core")).astype(BF) for i in (3, 4)]
    far_first, far_second = lax.optimization_barrier((far_first, far_second))
    half = far_first.shape[0]
    far_first, far_second = plane_shift(far_first, -1, 1), plane_shift(far_second, 1, 1)
    left, right = [total(mine[i], swap(other[i], "core")) for i in (1, 2)]
    left = jnp.concatenate([left[:half] + far_first.astype(F32), left[half:]]).astype(BF)
    right = jnp.concatenate([right[:half], right[half:] + far_second.astype(F32)]).astype(BF)
    left, right = lax.optimization_barrier((left, right))
    left, right = plane_shift(left, -1, 1), plane_shift(right, 1, 1)
    rows = total(mine[0], swap(other[0], "core"), left, right).astype(BF)
    rows = rows.reshape(4, -1, rows.shape[-1])
    near = [plane_shift(rows[i], by, 0) for i, by in ((1, -1), (2, 1), (3, 2))]
    return total(rows[0], *near).astype(BF)


STEPS = 2


def expert_kernel(count, *refs):
    rows_in, (gate_ref, up_ref, down_ref) = refs[:count], refs[count : count + 3]
    rows_out, (sums, hidden) = refs[count + 3 : 2 * count + 3], refs[2 * count + 3 :]
    step = pl.program_id(0)
    units = gate_ref.shape[1]

    def add(fresh):
        rows = jnp.concatenate([block[...] for block in rows_in])
        gate_val = jnp.dot(rows, gate_ref[...], preferred_element_type=F32)
        up_val = jnp.dot(rows, up_ref[...], preferred_element_type=F32)
        if fresh:
            sums[:, :units] = gate_val
            sums[:, units:] = up_val
        else:
            sums[:, :units] += gate_val
            sums[:, units:] += up_val

    pl.when(step == 0)(lambda: add(True))
    pl.when((step > 0) & (step < STEPS))(lambda: add(False))

    @pl.when(step == STEPS - 1)
    def _():
        gate_val, up_val = sums[:, :units], sums[:, units:]
        hidden[...] = (gate_val / (1.0 + jnp.exp(-gate_val)) * up_val).astype(BF)

    @pl.when(step >= STEPS)
    def _():
        result = jnp.dot(hidden[...], down_ref[...], preferred_element_type=F32).astype(BF)
        first = 0
        for block in rows_out:
            block[...] = result[first : first + block.shape[0]]
            first += block.shape[0]


def expert(blocks, gate_weight, up_weight, down_weight):
    features, units = gate_weight.shape
    rows = sum(block.shape[0] for block in blocks)
    wide = features // STEPS
    lead, trail = lambda i: jnp.minimum(i, STEPS - 1), lambda i: jnp.maximum(i - STEPS, 0)
    weight_in = pl.BlockSpec((wide, units), lambda i: (lead(i), 0))
    weight_out = pl.BlockSpec((units, wide), lambda i: (0, trail(i)))
    return pl.pallas_call(
        functools.partial(expert_kernel, len(blocks)),
        grid=(2 * STEPS,),
        in_specs=[pl.BlockSpec((b.shape[0], wide), lambda i: (0, lead(i))) for b in blocks]
        + [weight_in, weight_in, weight_out],
        out_specs=[pl.BlockSpec((b.shape[0], wide), lambda i: (0, trail(i))) for b in blocks],
        out_shape=[jax.ShapeDtypeStruct(b.shape, BF) for b in blocks],
        scratch_shapes=[pltpu.VMEM((rows, 2 * units), F32), pltpu.VMEM((rows, units), BF)],
        compiler_params=pltpu.CompilerParams(vmem_limit_bytes=40 * 1024 * 1024),
        cost_estimate=pl.CostEstimate(
            flops=6 * rows * features * units,
            bytes_accessed=2 * (3 * features * units + 2 * rows * features),
            transcendentals=rows * units,
        ),
        name="expert",
    )(*blocks, gate_weight, up_weight, down_weight)


def shards(
    queries,
    keys,
    values,
    segment_ids,
    residual,
    w_out,
    norm_gain,
    w_router,
    routes,
    w_gate,
    w_up,
    w_down,
):
    w_out_all = lax.all_gather(w_out, CTX, axis=1, tiled=True)
    attention = attend(queries, keys, values, segment_ids)
    head_partial = jnp.dot(attention, w_out_all, preferred_element_type=F32).astype(BF)
    width = head_partial.shape[1]
    tokens = routes.shape[0]

    route_flat = routes.reshape(-1)
    expert_ids = jnp.arange(EXPERTS, dtype=jnp.int32)
    onehot = (route_flat[:, None] == expert_ids).astype(jnp.int32)
    ranks = jnp.sum((jnp.cumsum(onehot, axis=0) - onehot) * onehot, axis=-1)
    slot_of_route = (route_flat * SLOTS + ranks).reshape(tokens, 2)
    slot_ids = jnp.arange(EXPERTS * SLOTS, dtype=jnp.int32)
    hot = slot_of_route[:, :, None] == slot_ids
    picks = jnp.any(hot, axis=1).astype(BF)
    head_partial, picks, hot = lax.optimization_barrier((head_partial, picks, hot))

    head_terms = lax.all_to_all(
        head_partial.reshape(16, tokens, width), EXP, split_axis=0, concat_axis=0, tiled=True
    )
    mixed = residual.astype(F32) + jnp.sum(head_terms.astype(F32), axis=0)
    normed = (
        mixed * lax.rsqrt(jnp.mean(mixed * mixed, axis=-1, keepdims=True) + EPSILON) * norm_gain
    ).astype(BF)

    outgoing = jnp.dot(picks.T, normed, preferred_element_type=F32).astype(BF)

    incoming = lax.all_to_all(
        outgoing.reshape(EXPERTS, SLOTS, width), "z", split_axis=0, concat_axis=0, tiled=True
    ).reshape(EXPERTS * SLOTS, width)
    mine, other = gather_plane(incoming)
    weights = w_gate[0], w_up[0], w_down[0]
    slot_sums = scatter_plane(expert(mine, *weights), expert(other, *weights))
    logits = jnp.dot(normed, w_router, preferred_element_type=F32)
    chosen = jnp.sum((routes[..., None] == expert_ids).astype(F32) * logits[:, None, :], axis=-1)
    gates = jax.nn.softmax(chosen, axis=-1)
    slot_gates = jnp.sum(jnp.where(hot, gates[:, :, None], 0.0), axis=1)
    slot_sums, slot_gates = lax.optimization_barrier((slot_sums, slot_gates))
    returned = lax.all_to_all(
        slot_sums.reshape(EXPERTS, SLOTS, width), "z", split_axis=0, concat_axis=0, tiled=True
    ).reshape(EXPERTS * SLOTS, width)

    mixture = jnp.dot(
        slot_gates,
        returned.astype(F32),
        precision=lax.Precision.HIGHEST,
        preferred_element_type=F32,
    )
    return (mixed + mixture).astype(BF)


def solution(mesh):
    fine = Mesh(mesh.devices.reshape(4, 2, 2, 8, 2), ("x", "yl", "core", "z", "yh"))
    both = CTX + EXP
    placed = (
        P(CTX, EXP),
        P(CTX, None),
        P(CTX, None),
        P(CTX),
        P(both, None),
        P(EXP, CTX),
        P(),
        P(),
        P(both, None),
        P(EXP, None, CTX),
        P(EXP, None, CTX),
        P(EXP, CTX, None),
    )
    return jax.shard_map(
        shards, mesh=fine, in_specs=placed, out_specs=P(both, None), check_vma=False
    )
```

profile of v0, /device:TPU:32, one launch (start us, length us, event | category | flops | bytes accessed | tf_op | source)
XLA Modules:
  0.0 257.7 jit_solution(11902690802434228803)
XLA Ops:
  6.5 0.7 all-gather.2.cloned.1.call-update
  7.3 0.8 constant_dynamic-slice_fusion
  8.1 0.7 convert_bitcast_fusion
  8.7 2.8 %collective-permute-start.1 = (bf16[136,256]{1,0:T(8,128)(2,1)S(1)}, bf16[136,256]{1,0:T(8,128)(2,1)S(1)}, u32[]{:S(2)}, u32[]{:S(2)}) collective-permute-start(bf16[136,256]{1,0:T(8,128)(2,1)S(1)} %get-tuple-element.53), channel_id=1, source_target_pairs={{0,192},{64,0},{128,64},{192,128},{1,193},{65,1},{129,65},{193,129... | collective-permute-start | bytes 208904 | tf_op jit(solution)/shard_map/ppermute | solution.py:68
  11.6 2.3 collective-permute-start.2
  13.9 0.8 copy.30
  15.1 2.9 %collective-permute-done = bf16[136,256]{1,0:T(8,128)(2,1)S(1)} collective-permute-done((bf16[136,256]{1,0:T(8,128)(2,1)S(1)}, bf16[136,256]{1,0:T(8,128)(2,1)S(1)}, u32[]{:S(2)}, u32[]{:S(2)}) %collective-permute-start) | collective-permute-done | bytes 69664 | tf_op jit(solution)/shard_map/ppermute | solution.py:68
  18.0 1.7 collective-permute-start.3
  20.1 5.3 %collective-permute-done.3 = bf16[4,136,256]{2,1,0:T(8,128)(2,1)S(1)} collective-permute-done((bf16[4,136,256]{2,1,0:T(8,128)(2,1)S(1)}, bf16[4,136,256]{2,1,0:T(8,128)(2,1)S(1)}, u32[]{:S(2)}, u32[]{:S(2)}) %collective-permute-start.3) | collective-permute-done | bytes 278560 | tf_op jit(solution)/shard_map/ppermute | solution.py:24
  25.6 1.8 collective-permute-done.4
  27.6 0.3 fusion.35
  27.9 0.3 copy-done.6
  28.2 1.3 compare_and_fusion
  29.5 1.6 fusion.36
  31.1 1.5 fusion.13
  32.6 20.8 %all-gather.2.cloned.1.call-done = bf16[384,6144]{1,0:T(8,128)(2,1)} async-done(((bf16[384,384]{1,0:T(8,128)(2,1)}), bf16[384,6144]{1,0:T(8,128)(2,1)}) %all-gather.2.cloned.1.call-update) | async-done | bytes 4718608 | tf_op jit(solution)/shard_map/all_gather | solution.py:205
  53.4 3.4 %convolution_convert_fusion = bf16[128,6144]{1,0:T(8,128)(2,1)S(1)} fusion(bf16[128,384]{0,1:T(8,128)(2,1)S(1)} %bitcast.92, bf16[384,6144]{1,0:T(8,128)(2,1)} %all-gather.2.cloned.1.call-done), kind=kOutput, calls=%fused_computation.1 | convolution fusion | flops 604766208 | bytes 6389760 | tf_op jit(solution)/shard_map/dot_general | solution.py:207
  56.8 48.6 %all_to_all.15 = bf16[16,8,6144]{2,1,0:T(8,128)(2,1)S(1)} all-to-all(bf16[16,8,6144]{2,1,0:T(8,128)(2,1)S(1)} %bitcast.84), channel_id=1, replica_groups=mesh['x'=4,'yl'=2,'core'=2,'z'=8,'yh'=2] {'z','yh'}, dimensions={0} | all-to-all | bytes 3145728 | tf_op jit(solution)/shard_map/all_to_all | solution.py:221
  105.6 0.7 copy-done.2
  106.5 0.3 convolution_convert_fusion.1
  107.0 18.8 %all_to_all.16 = bf16[8,3,6144]{2,1,0:T(4,128)(2,1)S(1)} all-to-all(bf16[8,3,6144]{2,1,0:T(4,128)(2,1)S(1)} %reshape.310), channel_id=1, replica_groups=mesh['x'=4,'yl'=2,'core'=2,'z'=8,'yh'=2] {'z'}, dimensions={0} | all-to-all | bytes 589824 | tf_op jit(solution)/shard_map/all_to_all | solution.py:231
  125.8 0.3 reshape.311
  126.1 2.6 %collective-permute-start.7 = (bf16[24,6144]{1,0:T(8,128)(2,1)S(1)}, bf16[24,6144]{1,0:T(8,128)(2,1)S(1)}, u32[]{:S(2)}, u32[]{:S(2)}) collective-permute-start(bf16[24,6144]{1,0:T(8,128)(2,1)S(1)} %reshape.311), channel_id=1, source_target_pairs={{0,128},{16,17},{32,160},{48,49},{1,129},{17,16},{33,161},{49,48},... | collective-permute-start | bytes 884744 | tf_op jit(solution)/shard_map/ppermute | solution.py:40
  128.7 1.7 collective-permute-start.6
  130.4 0.3 collective-permute-start.5
  130.7 7.6 %collective-permute-done.5 = bf16[24,6144]{1,0:T(8,128)(2,1)S(1)} collective-permute-done((bf16[24,6144]{1,0:T(8,128)(2,1)S(1)}, bf16[24,6144]{1,0:T(8,128)(2,1)S(1)}, u32[]{:S(2)}, u32[]{:S(2)}) %collective-permute-start.5) | collective-permute-done | bytes 294944 | tf_op jit(solution)/shard_map/ppermute | solution.py:40
  138.5 0.3 collective-permute-start.9
  138.7 2.0 collective-permute-start.8
  140.8 14.2 %collective-permute-done.9.refs_2_ = bf16[96,6144]{1,0:T(8,128)(2,1)S(1)} collective-permute-done((bf16[96,6144]{1,0:T(8,128)(2,1)S(1)}, bf16[96,6144]{1,0:T(8,128)(2,1)S(1)}, u32[]{:S(2)}, u32[]{:S(2)}) %collective-permute-start.9) | collective-permute-done | bytes 1179680 | tf_op jit(solution)/shard_map/ppermute | solution.py:40
  155.0 1.3 collective-permute-start.11
  156.3 0.9 collective-permute-start.10
  157.2 0.5 collective-permute-start.13
  157.7 7.2 %collective-permute-done.11.refs_4_ = bf16[48,6144]{1,0:T(8,128)(2,1)S(1)} collective-permute-done((bf16[48,6144]{1,0:T(8,128)(2,1)S(1)}, bf16[48,6144]{1,0:T(8,128)(2,1)S(1)}, u32[]{:S(2)}, u32[]{:S(2)}) %collective-permute-start.11) | collective-permute-done | bytes 589856 | tf_op jit(solution)/shard_map/ppermute | solution.py:40
  164.9 2.5 collective-permute-done.10.refs_3_
  167.5 2.0 collective-permute-done.15.refs_3_
  169.5 7.5 %expert.3 = (bf16[96,6144]{1,0:T(8,128)(2,1)S(1)}, bf16[96,6144]{1,0:T(8,128)(2,1)S(1)}, bf16[96,6144]{1,0:T(8,128)(2,1)S(1)}, bf16[48,6144]{1,0:T(8,128)(2,1)S(1)}, bf16[48,6144]{1,0:T(8,128)(2,1)S(1)}) custom-call(bf16[96,6144]{1,0:T(8,128)(2,1)S(1)} %collective-permute-done.12.refs_0_, bf16[96,6144]{1,0:T(8,128)(2,1)S(1)} %collective-permute-done.13.refs_1_, ...), custom_call_target="tpu_custom_call" | custom-call | flops 3623878656 | bytes 18874368 | tf_op jit(solution)/shard_map/expert/pallas_call | solution.py:173
  177.0 0.4 collective-permute-start.19
  177.5 7.5 %expert.2 = (bf16[96,6144]{1,0:T(8,128)(2,1)S(1)}, bf16[96,6144]{1,0:T(8,128)(2,1)S(1)}, bf16[96,6144]{1,0:T(8,128)(2,1)S(1)}, bf16[48,6144]{1,0:T(8,128)(2,1)S(1)}, bf16[48,6144]{1,0:T(8,128)(2,1)S(1)}) custom-call(bf16[96,6144]{1,0:T(8,128)(2,1)S(1)} %constant_dynamic-update-slice_fusion.refs_0_, bf16[96,6144]{1,0:T(8,128)(2,1)S(1)} %collective-permute-done.8.refs_1_, ...), custom_call_target="tpu_custom_call" | custom-call | flops 3623878656 | bytes 18874368 | tf_op jit(solution)/shard_map/expert/pallas_call | solution.py:173
  185.0 0.5 collective-permute-start.20
  185.6 0.4 collective-permute-start.18
  186.2 0.8 collective-permute-done.20
  187.2 0.8 collective-permute-start.21
  188.0 1.3 collective-permute-start.23
  189.3 1.1 collective-permute-done.18
  190.4 0.3 convert_add_fusion.1
  190.7 1.4 collective-permute-done.22
  192.1 0.3 convert_add_fusion
  192.5 4.6 %collective-permute-done.21 = bf16[48,6144]{1,0:T(8,128)(2,1)S(1)} collective-permute-done((bf16[48,6144]{1,0:T(8,128)(2,1)S(1)}, bf16[48,6144]{1,0:T(8,128)(2,1)S(1)}, u32[]{:S(2)}, u32[]{:S(2)}) %collective-permute-start.21) | collective-permute-done | bytes 589856 | tf_op jit(solution)/shard_map/ppermute | solution.py:40
  197.3 1.1 pad_maximum_fusion
  198.4 0.7 collective-permute-done.23
  199.2 1.1 pad_maximum_fusion.1
  200.3 1.3 collective-permute-start.24
  201.6 0.8 collective-permute-start.25
  202.7 14.1 %collective-permute-done.24 = bf16[96,6144]{1,0:T(8,128)(2,1)} collective-permute-done((bf16[96,6144]{1,0:T(8,128)(2,1)}, bf16[96,6144]{1,0:T(8,128)(2,1)}, u32[]{:S(2)}, u32[]{:S(2)}) %collective-permute-start.24) | collective-permute-done | bytes 1179680 | tf_op jit(solution)/shard_map/ppermute | solution.py:40
  216.8 2.5 collective-permute-done.25
  219.3 2.7 %add_convert_fusion = bf16[96,6144]{1,0:T(8,128)(2,1)S(1)} fusion(bf16[96,6144]{1,0:T(8,128)(2,1)} %collective-permute-done.25, bf16[96,6144]{1,0:T(8,128)(2,1)} %collective-permute-done.24, bf16[96,6144]{1,0:T(8,128)(2,1)} %collective-permute-done.17, bf16[96,6144]{1,0:T(8,128)(2,1)S(1)} %get-tuple-element.26), kind=kLoop, calls=%fused_computation.9 | loop fusion | flops 4718592 | bytes 5898240 | tf_op jit(solution)/shard_map/convert_element_type | solution.py:123
  222.1 1.1 collective-permute-start.26
  223.2 1.6 collective-permute-start.28
  224.8 0.8 collective-permute-start.27
  225.7 3.1 %collective-permute-done.26 = bf16[24,6144]{1,0:T(8,128)(2,1)S(1)} collective-permute-done((bf16[24,6144]{1,0:T(8,128)(2,1)S(1)}, bf16[24,6144]{1,0:T(8,128)(2,1)S(1)}, u32[]{:S(2)}, u32[]{:S(2)}) %collective-permute-start.26) | collective-permute-done | bytes 294944 | tf_op jit(solution)/shard_map/ppermute | solution.py:40
  228.9 2.7 %collective-permute-done.28 = bf16[24,6144]{1,0:T(8,128)(2,1)S(1)} collective-permute-done((bf16[24,6144]{1,0:T(8,128)(2,1)S(1)}, bf16[24,6144]{1,0:T(8,128)(2,1)S(1)}, u32[]{:S(2)}, u32[]{:S(2)}) %collective-permute-start.28) | collective-permute-done | bytes 294944 | tf_op jit(solution)/shard_map/ppermute | solution.py:40
  231.5 3.1 %collective-permute-done.27 = bf16[24,6144]{1,0:T(8,128)(2,1)S(1)} collective-permute-done((bf16[24,6144]{1,0:T(8,128)(2,1)S(1)}, bf16[24,6144]{1,0:T(8,128)(2,1)S(1)}, u32[]{:S(2)}, u32[]{:S(2)}) %collective-permute-start.27) | collective-permute-done | bytes 294944 | tf_op jit(solution)/shard_map/ppermute | solution.py:40
  234.9 14.8 %all_to_all.17 = bf16[8,3,6144]{2,1,0:T(4,128)(2,1)S(1)} all-to-all(bf16[8,3,6144]{2,1,0:T(4,128)(2,1)S(1)} %reshape.312), channel_id=1, replica_groups=mesh['x'=4,'yl'=2,'core'=2,'z'=8,'yh'=2] {'z'}, dimensions={0} | all-to-all | bytes 589824 | tf_op jit(solution)/shard_map/all_to_all | solution.py:242
  249.9 0.9 fusion.1
  (78 shorter events, 4.1 us)
Async XLA Ops:
  6.5 195.8 %copy-start = (bf16[6144,8]{0,1:T(8,128)(2,1)S(1)}, bf16[6144,8]{0,1:T(8,128)(2,1)}, u32[]{:S(2)}) copy-start(bf16[6144,8]{0,1:T(8,128)(2,1)} %param.19) | copy-start | bytes 294916
  6.5 13.3 %copy-start.3 = (bf16[128,384]{1,0:T(8,128)(2,1)S(1)}, bf16[128,384]{1,0:T(8,128)(2,1)}, u32[]{:S(2)}) copy-start(bf16[128,384]{1,0:T(8,128)(2,1)} %param.12) | copy-start | bytes 294916
  6.5 46.9 %all-gather.2.cloned.1.call-start = ((), (), s32[]{:S(2)}) async-start(), calls=%async_computation.3 | async-start | bytes 5013504 | tf_op jit(solution)/shard_map/all_gather | solution.py:205
  8.7 6.3 %collective-permute-start.1 = (bf16[136,256]{1,0:T(8,128)(2,1)S(1)}, bf16[136,256]{1,0:T(8,128)(2,1)S(1)}, u32[]{:S(2)}, u32[]{:S(2)}) collective-permute-start(bf16[136,256]{1,0:T(8,128)(2,1)S(1)} %get-tuple-element.53), channel_id=1, source_target_pairs={{0,192},{64,0},{128,64},{192,128},{1,193},{65,1},{129,65},{193,129... | collective-permute-start | bytes 208904 | tf_op jit(solution)/shard_map/ppermute | solution.py:68
  11.6 6.4 %collective-permute-start = (bf16[136,256]{1,0:T(8,128)(2,1)S(1)}, bf16[136,256]{1,0:T(8,128)(2,1)S(1)}, u32[]{:S(2)}, u32[]{:S(2)}) collective-permute-start(bf16[136,256]{1,0:T(8,128)(2,1)S(1)} %get-tuple-element.53), channel_id=1, source_target_pairs={{0,64},{64,128},{128,192},{192,0},{1,65},{65,129},{129,193},{193,1... | collective-permute-start | bytes 208904 | tf_op jit(solution)/shard_map/ppermute | solution.py:68
  11.6 6.4 %collective-permute-start.2 = (bf16[136,256]{1,0:T(8,128)(2,1)S(1)}, bf16[136,256]{1,0:T(8,128)(2,1)S(1)}, u32[]{:S(2)}, u32[]{:S(2)}) collective-permute-start(bf16[136,256]{1,0:T(8,128)(2,1)S(1)} %get-tuple-element.53), channel_id=1, source_target_pairs={{0,128},{64,192},{128,0},{192,64},{1,129},{65,193},{129,1},{193,65... | collective-permute-start | bytes 208904 | tf_op jit(solution)/shard_map/ppermute | solution.py:68
  18.0 7.3 %collective-permute-start.3 = (bf16[4,136,256]{2,1,0:T(8,128)(2,1)S(1)}, bf16[4,136,256]{2,1,0:T(8,128)(2,1)S(1)}, u32[]{:S(2)}, u32[]{:S(2)}) collective-permute-start(bf16[4,136,256]{2,1,0:T(8,128)(2,1)S(1)} %get-tuple-element.51), channel_id=1, source_target_pairs={{0,32},{32,0},{1,33},{33,1},{2,34},{34,2},{3,35},{35,3},{4,36},{36... | collective-permute-start | bytes 835592 | tf_op jit(solution)/shard_map/ppermute | solution.py:24
  25.4 2.0 collective-permute-start.4
  27.6 0.7 copy-start.6
  105.4 0.9 copy-start.2
  105.4 1.1 copy-start.4
  126.1 12.3 %collective-permute-start.7 = (bf16[24,6144]{1,0:T(8,128)(2,1)S(1)}, bf16[24,6144]{1,0:T(8,128)(2,1)S(1)}, u32[]{:S(2)}, u32[]{:S(2)}) collective-permute-start(bf16[24,6144]{1,0:T(8,128)(2,1)S(1)} %reshape.311), channel_id=1, source_target_pairs={{0,128},{16,17},{32,160},{48,49},{1,129},{17,16},{33,161},{49,48},... | collective-permute-start | bytes 884744 | tf_op jit(solution)/shard_map/ppermute | solution.py:40
  128.7 9.7 %collective-permute-start.6 = (bf16[24,6144]{1,0:T(8,128)(2,1)S(1)}, bf16[24,6144]{1,0:T(8,128)(2,1)S(1)}, u32[]{:S(2)}, u32[]{:S(2)}) collective-permute-start(bf16[24,6144]{1,0:T(8,128)(2,1)S(1)} %reshape.311), channel_id=1, source_target_pairs={{0,192},{16,49},{32,224},{48,16},{1,193},{17,48},{33,225},{49,17},... | collective-permute-start | bytes 884744 | tf_op jit(solution)/shard_map/ppermute | solution.py:40
  130.4 7.9 %collective-permute-start.5 = (bf16[24,6144]{1,0:T(8,128)(2,1)S(1)}, bf16[24,6144]{1,0:T(8,128)(2,1)S(1)}, u32[]{:S(2)}, u32[]{:S(2)}) collective-permute-start(bf16[24,6144]{1,0:T(8,128)(2,1)S(1)} %reshape.311), channel_id=1, source_target_pairs={{0,64},{16,48},{32,96},{48,17},{1,65},{17,49},{33,97},{49,16},{64,... | collective-permute-start | bytes 884744 | tf_op jit(solution)/shard_map/ppermute | solution.py:40
  138.4 31.1 %copy-start.1 = (bf16[1,6144,256]{2,1,0:T(8,128)(2,1)S(1)}, bf16[1,6144,256]{2,1,0:T(8,128)(2,1)}, u32[]{:S(2)}) copy-start(bf16[1,6144,256]{2,1,0:T(8,128)(2,1)} %param.21) | copy-start | bytes 9437188
  138.5 16.5 %collective-permute-start.9 = (bf16[96,6144]{1,0:T(8,128)(2,1)S(1)}, bf16[96,6144]{1,0:T(8,128)(2,1)S(1)}, u32[]{:S(2)}, u32[]{:S(2)}) collective-permute-start(bf16[96,6144]{1,0:T(8,128)(2,1)S(1)} %constant_dynamic-update-slice_fusion.refs_0_), channel_id=1, source_target_pairs={{0,33},{16,208},{32,0},{48,240},{1,32},{17,209},{33,1},{49,241},{6... | collective-permute-start | bytes 3538952 | tf_op jit(solution)/shard_map/ppermute | solution.py:40
  138.7 17.5 %collective-permute-start.8 = (bf16[96,6144]{1,0:T(8,128)(2,1)S(1)}, bf16[96,6144]{1,0:T(8,128)(2,1)S(1)}, u32[]{:S(2)}, u32[]{:S(2)}) collective-permute-start(bf16[96,6144]{1,0:T(8,128)(2,1)S(1)} %constant_dynamic-update-slice_fusion.refs_0_), channel_id=1, source_target_pairs={{0,32},{16,80},{32,1},{48,112},{1,33},{17,81},{33,0},{49,113},{64,... | collective-permute-start | bytes 3538952 | tf_op jit(solution)/shard_map/ppermute | solution.py:40
  140.8 26.7 %collective-permute-start.12 = (bf16[96,6144]{1,0:T(8,128)(2,1)S(1)}, bf16[96,6144]{1,0:T(8,128)(2,1)S(1)}, u32[]{:S(2)}, u32[]{:S(2)}) collective-permute-start(bf16[96,6144]{1,0:T(8,128)(2,1)S(1)} %constant_dynamic-update-slice_fusion.refs_0_), channel_id=1, source_target_pairs={{0,16},{16,0},{1,17},{17,1},{2,18},{18,2},{3,19},{19,3},{4,20},{20... | collective-permute-start | bytes 3538952 | tf_op jit(solution)/shard_map/ppermute | solution.py:24
  155.0 10.0 %collective-permute-start.11 = (bf16[48,6144]{1,0:T(8,128)(2,1)S(1)}, bf16[48,6144]{1,0:T(8,128)(2,1)S(1)}, u32[]{:S(2)}, u32[]{:S(2)}) collective-permute-start(bf16[48,6144]{1,0:T(8,128)(2,1)S(1)} %slice.62), channel_id=1, source_target_pairs={{0,33},{16,208},{32,0},{48,240},{1,32},{17,209},{33,1},{49,241},{6... | collective-permute-start | bytes 1769480 | tf_op jit(solution)/shard_map/ppermute | solution.py:40
  156.3 11.2 %collective-permute-start.10 = (bf16[48,6144]{1,0:T(8,128)(2,1)S(1)}, bf16[48,6144]{1,0:T(8,128)(2,1)S(1)}, u32[]{:S(2)}, u32[]{:S(2)}) collective-permute-start(bf16[48,6144]{1,0:T(8,128)(2,1)S(1)} %slice.61), channel_id=1, source_target_pairs={{0,32},{16,80},{32,1},{48,112},{1,33},{17,81},{33,0},{49,113},{64,... | collective-permute-start | bytes 1769480 | tf_op jit(solution)/shard_map/ppermute | solution.py:40
  157.2 12.3 %collective-permute-start.14 = (bf16[96,6144]{1,0:T(8,128)(2,1)S(1)}, bf16[96,6144]{1,0:T(8,128)(2,1)S(1)}, u32[]{:S(2)}, u32[]{:S(2)}) collective-permute-start(bf16[96,6144]{1,0:T(8,128)(2,1)S(1)} %collective-permute-done.9.refs_2_), channel_id=1, source_target_pairs={{0,16},{16,0},{1,17},{17,1},{2,18},{18,2},{3,19},{19,3},{4,20},{20... | collective-permute-start | bytes 3538952 | tf_op jit(solution)/shard_map/ppermute | solution.py:24
  157.2 12.3 %collective-permute-start.13 = (bf16[96,6144]{1,0:T(8,128)(2,1)S(1)}, bf16[96,6144]{1,0:T(8,128)(2,1)S(1)}, u32[]{:S(2)}, u32[]{:S(2)}) collective-permute-start(bf16[96,6144]{1,0:T(8,128)(2,1)S(1)} %collective-permute-done.8.refs_1_), channel_id=1, source_target_pairs={{0,16},{16,0},{1,17},{17,1},{2,18},{18,2},{3,19},{19,3},{4,20},{20... | collective-permute-start | bytes 3538952 | tf_op jit(solution)/shard_map/ppermute | solution.py:24
  164.9 2.6 collective-permute-start.16
  167.5 2.0 collective-permute-start.15
  177.0 9.1 %collective-permute-start.19 = (bf16[48,6144]{1,0:T(8,128)(2,1)S(1)}, bf16[48,6144]{1,0:T(8,128)(2,1)S(1)}, u32[]{:S(2)}, u32[]{:S(2)}) collective-permute-start(bf16[48,6144]{1,0:T(8,128)(2,1)S(1)} %get-tuple-element.31), channel_id=1, source_target_pairs={{0,16},{16,0},{1,17},{17,1},{2,18},{18,2},{3,19},{19,3},{4,20},{20... | collective-permute-start | bytes 1769480 | tf_op jit(solution)/shard_map/ppermute | solution.py:24
  185.0 2.1 collective-permute-start.20
  185.4 17.3 %collective-permute-start.17 = (bf16[96,6144]{1,0:T(8,128)(2,1)S(1)}, bf16[96,6144]{1,0:T(8,128)(2,1)}, u32[]{:S(2)}, u32[]{:S(2)}) collective-permute-start(bf16[96,6144]{1,0:T(8,128)(2,1)S(1)} %get-tuple-element.27), channel_id=1, source_target_pairs={{0,16},{16,0},{1,17},{17,1},{2,18},{18,2},{3,19},{19,3},{4,20},{20... | collective-permute-start | bytes 3538952 | tf_op jit(solution)/shard_map/ppermute | solution.py:24
  185.6 4.9 %collective-permute-start.18 = (bf16[96,6144]{1,0:T(8,128)(2,1)S(1)}, bf16[96,6144]{1,0:T(8,128)(2,1)S(1)}, u32[]{:S(2)}, u32[]{:S(2)}) collective-permute-start(bf16[96,6144]{1,0:T(8,128)(2,1)S(1)} %get-tuple-element.29), channel_id=1, source_target_pairs={{0,16},{16,0},{1,17},{17,1},{2,18},{18,2},{3,19},{19,3},{4,20},{20... | collective-permute-start | bytes 3538952 | tf_op jit(solution)/shard_map/ppermute | solution.py:24
  185.9 6.2 %collective-permute-start.22 = (bf16[96,6144]{1,0:T(8,128)(2,1)S(1)}, bf16[96,6144]{1,0:T(8,128)(2,1)S(1)}, u32[]{:S(2)}, u32[]{:S(2)}) collective-permute-start(bf16[96,6144]{1,0:T(8,128)(2,1)S(1)} %get-tuple-element.36), channel_id=1, source_target_pairs={{0,16},{16,0},{1,17},{17,1},{2,18},{18,2},{3,19},{19,3},{4,20},{20... | collective-permute-start | bytes 3538952 | tf_op jit(solution)/shard_map/ppermute | solution.py:24
  187.2 10.0 %collective-permute-start.21 = (bf16[48,6144]{1,0:T(8,128)(2,1)S(1)}, bf16[48,6144]{1,0:T(8,128)(2,1)S(1)}, u32[]{:S(2)}, u32[]{:S(2)}) collective-permute-start(bf16[48,6144]{1,0:T(8,128)(2,1)S(1)} %add_convert_fusion.2), channel_id=1, source_target_pairs={{0,33},{16,208},{32,0},{48,240},{1,32},{17,209},{33,1},{49,241},{6... | collective-permute-start | bytes 1769480 | tf_op jit(solution)/shard_map/ppermute | solution.py:40
  188.0 11.1 %collective-permute-start.23 = (bf16[48,6144]{1,0:T(8,128)(2,1)S(1)}, bf16[48,6144]{1,0:T(8,128)(2,1)S(1)}, u32[]{:S(2)}, u32[]{:S(2)}) collective-permute-start(bf16[48,6144]{1,0:T(8,128)(2,1)S(1)} %add_convert_fusion.1), channel_id=1, source_target_pairs={{0,32},{16,80},{32,1},{48,112},{1,33},{17,81},{33,0},{49,113},{64,... | collective-permute-start | bytes 1769480 | tf_op jit(solution)/shard_map/ppermute | solution.py:40
  199.2 3.3 %copy-start.5 = (s32[8,2]{0,1:T(2,128)S(1)}, s32[8,2]{0,1:T(2,128)}, u32[]{:S(2)}) copy-start(s32[8,2]{0,1:T(2,128)} %param.20) | copy-start | bytes 196
  200.3 16.5 %collective-permute-start.24 = (bf16[96,6144]{1,0:T(8,128)(2,1)}, bf16[96,6144]{1,0:T(8,128)(2,1)}, u32[]{:S(2)}, u32[]{:S(2)}) collective-permute-start(bf16[96,6144]{1,0:T(8,128)(2,1)} %pad_maximum_fusion), channel_id=1, source_target_pairs={{0,33},{16,208},{32,0},{48,240},{1,32},{17,209},{33,1},{49,241},{6... | collective-permute-start | bytes 3538952 | tf_op jit(solution)/shard_map/ppermute | solution.py:40
  201.6 17.7 %collective-permute-start.25 = (bf16[96,6144]{1,0:T(8,128)(2,1)}, bf16[96,6144]{1,0:T(8,128)(2,1)}, u32[]{:S(2)}, u32[]{:S(2)}) collective-permute-start(bf16[96,6144]{1,0:T(8,128)(2,1)} %pad_maximum_fusion.1), channel_id=1, source_target_pairs={{0,32},{16,80},{32,1},{48,112},{1,33},{17,81},{33,0},{49,113},{64,... | collective-permute-start | bytes 3538952 | tf_op jit(solution)/shard_map/ppermute | solution.py:40
  222.1 6.8 %collective-permute-start.26 = (bf16[24,6144]{1,0:T(8,128)(2,1)S(1)}, bf16[24,6144]{1,0:T(8,128)(2,1)S(1)}, u32[]{:S(2)}, u32[]{:S(2)}) collective-permute-start(bf16[24,6144]{1,0:T(8,128)(2,1)S(1)} %get-tuple-element.43), channel_id=1, source_target_pairs={{0,192},{16,49},{32,224},{48,16},{1,193},{17,48},{33,225},{49,17},... | collective-permute-start | bytes 884744 | tf_op jit(solution)/shard_map/ppermute | solution.py:40
  223.2 8.3 %collective-permute-start.28 = (bf16[24,6144]{1,0:T(8,128)(2,1)S(1)}, bf16[24,6144]{1,0:T(8,128)(2,1)S(1)}, u32[]{:S(2)}, u32[]{:S(2)}) collective-permute-start(bf16[24,6144]{1,0:T(8,128)(2,1)S(1)} %get-tuple-element.44), channel_id=1, source_target_pairs={{0,128},{16,17},{32,160},{48,49},{1,129},{17,16},{33,161},{49,48},... | collective-permute-start | bytes 884744 | tf_op jit(solution)/shard_map/ppermute | solution.py:40
  224.8 9.8 %collective-permute-start.27 = (bf16[24,6144]{1,0:T(8,128)(2,1)S(1)}, bf16[24,6144]{1,0:T(8,128)(2,1)S(1)}, u32[]{:S(2)}, u32[]{:S(2)}) collective-permute-start(bf16[24,6144]{1,0:T(8,128)(2,1)S(1)} %get-tuple-element.45), channel_id=1, source_target_pairs={{0,64},{16,48},{32,96},{48,17},{1,65},{17,49},{33,97},{49,16},{64,... | collective-permute-start | bytes 884744 | tf_op jit(solution)/shard_map/ppermute | solution.py:40
Sparse Core Ops, SparseCore 0:
  9.2 44.1 all-gather.1
where the time goes:
time: 258 us
  waiting for transfers between devices  99.1 us (38%)
  blocking collectives  82.2 us (32%)
  starting transfers between devices  25.8 us (10%)
  Pallas kernels  15 us (6%)
  between operations  13.8 us (5%)
  other arithmetic  9.54 us (4%)
  matrix products  7.8 us (3%)
  local copies, waits for them, and re-layouts  4.52 us (2%)
    ppermute x14, waiting for transfers between devices, plane_shift(): return lax.ppermute(value, PLANE, pairs)  62.3 us
    all_to_all x1, blocking collectives, shards(): lax.all_to_all(head_partial.reshape(16, tokens, width), EXP, split_axis=0...  48.6 us
    all_gather x1, waiting for transfers between devices, shards(): w_out_all = lax.all_gather(w_out, CTX, axis=1, tiled=True)  20.8 us
    all_to_all x1, blocking collectives, shards(): lax.all_to_all(outgoing.reshape(EXPERTS, SLOTS, width), 'z', split_axis=0...  18.8 us
    ppermute x14, starting transfers between devices, plane_shift(): return lax.ppermute(value, PLANE, pairs)  16.8 us
    pallas_call x2, Pallas kernels, expert(): pl.pallas_call(functools.partial(expert_kernel, len(blocks)), grid=(2 * S...  15 us
    all_to_all x1, blocking collectives, shards(): lax.all_to_all(slot_sums.reshape(EXPERTS, SLOTS, width), 'z', split_axis=...  14.8 us
    ppermute x12, waiting for transfers between devices, swap(): return lax.ppermute(value, axis, [(0, 1), (1, 0)])  12.5 us
  transfers between devices with their start and end apart: 30, of which 19 were waited for; matrix products, arithmetic and copies ran while one was open for 5% of the time, Pallas kernels for 3%

commit v1 on v0

--- a/solution.py
+++ b/solution.py
@@ -99,15 +99,20 @@
     return attention.transpose(1, 0, 2).reshape(rows, head_count * HD)
 
 
-def gather_plane(rows):
+def plane_experts(rows, expert_of):
     near = [plane_shift(rows, by, 0) for by in (1, -1, 2)]
     rows = jnp.concatenate([rows] + near)
     half = rows.shape[0] // 2
     left, right = plane_shift(rows, 1, 1), plane_shift(rows, -1, 1)
     far_first = plane_shift(left[:half], 1, 1)
     far_second = plane_shift(right[half:], -1, 1)
-    mine = [rows, left, right, far_first, far_second]
-    return mine, [swap(block, "core") for block in mine]
+    mine = [rows, left, right]
+    other = [swap(block, "core") for block in mine]
+    near = expert_of(mine)
+    far_first, far_second, first = lax.optimization_barrier((far_first, far_second, near[0]))
+    far = [far_first, far_second]
+    rest = expert_of(far + other + [swap(block, "core") for block in far])
+    return [first, *near[1:], *rest[:2]], rest[2:]
 
 
 def scatter_plane(mine, other):
@@ -115,9 +120,9 @@
     far_first, far_second = lax.optimization_barrier((far_first, far_second))
     half = far_first.shape[0]
     far_first, far_second = plane_shift(far_first, -1, 1), plane_shift(far_second, 1, 1)
-    left, right = [total(mine[i], swap(other[i], "core")) for i in (1, 2)]
-    left = jnp.concatenate([left[:half] + far_first.astype(F32), left[half:]]).astype(BF)
-    right = jnp.concatenate([right[:half], right[half:] + far_second.astype(F32)]).astype(BF)
+    left = total(mine[1], swap(other[1], "core"), jnp.pad(far_first, ((0, half), (0, 0))))
+    right = total(mine[2], swap(other[2], "core"), jnp.pad(far_second, ((half, 0), (0, 0))))
+    left, right = left.astype(BF), right.astype(BF)
     left, right = lax.optimization_barrier((left, right))
     left, right = plane_shift(left, -1, 1), plane_shift(right, 1, 1)
     rows = total(mine[0], swap(other[0], "core"), left, right).astype(BF)
@@ -216,12 +221,16 @@
     slot_ids = jnp.arange(EXPERTS * SLOTS, dtype=jnp.int32)
     hot = slot_of_route[:, :, None] == slot_ids
     picks = jnp.any(hot, axis=1).astype(BF)
-    head_partial, picks, hot = lax.optimization_barrier((head_partial, picks, hot))
+    yh = lax.axis_index("yh")
+    head_partial, picks, hot, yh = lax.optimization_barrier((head_partial, picks, hot, yh))
 
     head_terms = lax.all_to_all(
-        head_partial.reshape(16, tokens, width), EXP, split_axis=0, concat_axis=0, tiled=True
-    )
-    mixed = residual.astype(F32) + jnp.sum(head_terms.astype(F32), axis=0)
+        head_partial.reshape(8, 2 * tokens, width), "z", split_axis=0, concat_axis=0, tiled=True
+    )
+    head_sums = jnp.sum(head_terms.astype(F32), axis=0).reshape(2, tokens, width)
+    own_sum = lax.dynamic_index_in_dim(head_sums, yh, 0, keepdims=False)
+    sent = lax.dynamic_index_in_dim(head_sums, 1 - yh, 0, keepdims=False).astype(BF)
+    mixed = residual.astype(F32) + own_sum + swap(sent, "yh").astype(F32)
     normed = (
         mixed * lax.rsqrt(jnp.mean(mixed * mixed, axis=-1, keepdims=True) + EPSILON) * norm_gain
     ).astype(BF)
@@ -231,9 +240,9 @@
     incoming = lax.all_to_all(
         outgoing.reshape(EXPERTS, SLOTS, width), "z", split_axis=0, concat_axis=0, tiled=True
     ).reshape(EXPERTS * SLOTS, width)
-    mine, other = gather_plane(incoming)
     weights = w_gate[0], w_up[0], w_down[0]
-    slot_sums = scatter_plane(expert(mine, *weights), expert(other, *weights))
+    mine, other = plane_experts(incoming, lambda blocks: expert(blocks, *weights))
+    slot_sums = scatter_plane(mine, other)
     logits = jnp.dot(normed, w_router, preferred_element_type=F32)
     chosen = jnp.sum((routes[..., None] == expert_ids).astype(F32) * logits[:, None, :], axis=-1)
     gates = jax.nn.softmax(chosen, axis=-1)

time: 258 us -> 266 us (1.031)
  blocking collectives: 82.2 us -> 31.1 us
  waiting for transfers between devices: 99.1 us -> 133 us
  starting transfers between devices: 25.8 us -> 42.7 us
  local copies, waits for them, and re-layouts: 4.52 us -> 9.3 us
    all_to_all x1 -> x0, blocking collectives: 48.6 us -> none  [shards(): lax.all_to_all(head_partial.reshape(16, tokens, width), EXP, split_axis=0...]
    all_to_all x0 -> x1, waiting for transfers between devices: none -> 38.9 us  [shards(): lax.all_to_all(head_partial.reshape(8, 2 * tokens, width), 'z', split_axi...]
    all_to_all x0 -> x1, starting transfers between devices: none -> 7.75 us  [shards(): lax.all_to_all(head_partial.reshape(8, 2 * tokens, width), 'z', split_axi...]
    ppermute x14, waiting for transfers between devices: 62.3 us -> 54.5 us  [plane_shift(): return lax.ppermute(value, PLANE, pairs)]
    ppermute x14, starting transfers between devices: 16.8 us -> 22 us  [plane_shift(): return lax.ppermute(value, PLANE, pairs)]
    ppermute x12 -> x13, starting transfers between devices: 3.83 us -> 7.82 us  [swap(): return lax.ppermute(value, axis, [(0, 1), (1, 0)])]
    ppermute x12 -> x13, waiting for transfers between devices: 12.5 us -> 16.1 us  [swap(): return lax.ppermute(value, axis, [(0, 1), (1, 0)])]
    all_to_all x1, blocking collectives: 18.8 us -> 15.8 us  [shards(): lax.all_to_all(outgoing.reshape(EXPERTS, SLOTS, width), 'z', split_axis=0...]
  transfers between devices with their start and end apart: 30 -> 32, of which waited for: 19 -> 22; matrix products, arithmetic and copies ran while one was open for 5% -> 5% of each run, Pallas kernels for 3% -> 2%
where the time goes in v1:
time: 266 us; the launch traced here: 264 us
  waiting for transfers between devices  133 us (50%)
  starting transfers between devices  42.7 us (16%)
  blocking collectives  31.1 us (12%)
  Pallas kernels  15 us (6%)
  between operations  13.7 us (5%)
  matrix products  9.81 us (4%)
  local copies, waits for them, and re-layouts  9.3 us (3%)
  other arithmetic  9.23 us (3%)
    ppermute x14, waiting for transfers between devices, plane_shift(): return lax.ppermute(value, PLANE, pairs)  54.5 us
    all_to_all x1, waiting for transfers between devices, shards(): lax.all_to_all(head_partial.reshape(8, 2 * tokens, width), 'z', split_axi...  38.9 us
    ppermute x14, starting transfers between devices, plane_shift(): return lax.ppermute(value, PLANE, pairs)  22 us
    all_gather x1, waiting for transfers between devices, shards(): w_out_all = lax.all_gather(w_out, CTX, axis=1, tiled=True)  19.4 us
    ppermute x13, waiting for transfers between devices, swap(): return lax.ppermute(value, axis, [(0, 1), (1, 0)])  16.1 us
    all_to_all x1, blocking collectives, shards(): lax.all_to_all(outgoing.reshape(EXPERTS, SLOTS, width), 'z', split_axis=0...  15.8 us
    all_to_all x1, blocking collectives, shards(): lax.all_to_all(slot_sums.reshape(EXPERTS, SLOTS, width), 'z', split_axis=...  15.3 us
    pallas_call x2, Pallas kernels, expert(): pl.pallas_call(functools.partial(expert_kernel, len(blocks)), grid=(2 * S...  15 us
  transfers between devices with their start and end apart: 32, of which 22 were waited for; matrix products, arithmetic and copies ran while one was open for 5% of the time, Pallas kernels for 2%

profile of v1, /device:TPU:32, one launch (start us, length us, event | category | flops | bytes accessed | tf_op | source)
XLA Modules:
  0.0 263.9 jit_solution(11395088902073106945)
XLA Ops:
  6.5 0.7 all-gather.2.cloned.1.call-update
  7.3 0.8 constant_dynamic-slice_fusion
  8.1 0.7 convert_bitcast_fusion
  8.7 3.1 %collective-permute-start.2 = (bf16[136,256]{1,0:T(8,128)(2,1)S(1)}, bf16[136,256]{1,0:T(8,128)(2,1)S(1)}, u32[]{:S(2)}, u32[]{:S(2)}) collective-permute-start(bf16[136,256]{1,0:T(8,128)(2,1)S(1)} %get-tuple-element.63), channel_id=1, source_target_pairs={{0,128},{64,192},{128,0},{192,64},{1,129},{65,193},{129,1},{193,65... | collective-permute-start | bytes 208904 | tf_op jit(solution)/shard_map/ppermute | solution.py:68
  11.8 1.1 collective-permute-start.1
  13.0 0.9 collective-permute-start
  13.9 0.8 copy.30
  15.1 1.1 collective-permute-done.1
  16.2 2.3 collective-permute-done
  18.6 1.7 collective-permute-start.3
  20.6 5.5 %collective-permute-done.3 = bf16[4,136,256]{2,1,0:T(8,128)(2,1)S(1)} collective-permute-done((bf16[4,136,256]{2,1,0:T(8,128)(2,1)S(1)}, bf16[4,136,256]{2,1,0:T(8,128)(2,1)S(1)}, u32[]{:S(2)}, u32[]{:S(2)}) %collective-permute-start.3) | collective-permute-done | bytes 278560 | tf_op jit(solution)/shard_map/ppermute | solution.py:24
  26.4 1.9 collective-permute-done.4
  28.7 0.3 copy-done.9
  29.1 1.3 compare_and_fusion
  30.4 1.5 fusion.38
  31.9 1.6 fusion.11
  33.5 19.4 %all-gather.2.cloned.1.call-done = bf16[384,6144]{1,0:T(8,128)(2,1)} async-done(((bf16[384,384]{1,0:T(8,128)(2,1)}), bf16[384,6144]{1,0:T(8,128)(2,1)}) %all-gather.2.cloned.1.call-update) | async-done | bytes 4718608 | tf_op jit(solution)/shard_map/all_gather | solution.py:210
  52.8 4.6 %convolution_convert_fusion = bf16[128,6144]{1,0:T(8,128)(2,1)} fusion(bf16[128,384]{0,1:T(8,128)(2,1)S(1)} %bitcast.99, bf16[384,6144]{1,0:T(8,128)(2,1)} %all-gather.2.cloned.1.call-done), kind=kOutput, calls=%fused_computation.1 | convolution fusion | flops 604766208 | bytes 6389760 | tf_op jit(solution)/shard_map/dot_general | solution.py:212
  57.4 7.8 %all-to-all-start = ((bf16[8,16,6144]{2,1,0:T(8,128)(2,1)}), bf16[8,16,6144]{2,1,0:T(8,128)(2,1)S(1)}, u32[]{:S(2)}, u32[]{:S(2)}) async-start(bf16[8,16,6144]{2,1,0:T(8,128)(2,1)} %bitcast.37), calls=%async_computation | async-start | bytes 3145728 | tf_op jit(solution)/shard_map/all_to_all | solution.py:227
  65.2 38.9 %all-to-all-done = bf16[8,16,6144]{2,1,0:T(8,128)(2,1)S(1)} async-done(((bf16[8,16,6144]{2,1,0:T(8,128)(2,1)}), bf16[8,16,6144]{2,1,0:T(8,128)(2,1)S(1)}, u32[]{:S(2)}, u32[]{:S(2)}) %all-to-all-start) | async-done | bytes 1572896 | tf_op jit(solution)/shard_map/all_to_all | solution.py:227
  104.3 3.3 %collective-permute-start.5 = (bf16[8,6144]{1,0:T(8,128)(2,1)S(1)}, bf16[8,6144]{1,0:T(8,128)(2,1)S(1)}, u32[]{:S(2)}, u32[]{:S(2)}) collective-permute-start(bf16[8,6144]{1,0:T(8,128)(2,1)S(1)} %fusion.16), channel_id=1, source_target_pairs={{0,1},{1,0},{2,3},{3,2},{4,5},{5,4},{6,7},{7,6},{8,9},{9,8},{10,11... | collective-permute-start | bytes 294920 | tf_op jit(solution)/shard_map/ppermute | solution.py:24
  107.6 2.9 %collective-permute-done.5 = bf16[8,6144]{1,0:T(8,128)(2,1)S(1)} collective-permute-done((bf16[8,6144]{1,0:T(8,128)(2,1)S(1)}, bf16[8,6144]{1,0:T(8,128)(2,1)S(1)}, u32[]{:S(2)}, u32[]{:S(2)}) %collective-permute-start.5) | collective-permute-done | bytes 98336 | tf_op jit(solution)/shard_map/ppermute | solution.py:24
  110.7 1.0 convolution_convert_fusion.1
  111.7 2.0 reshape.315
  113.7 15.8 %all_to_all.15 = bf16[8,3,6144]{2,1,0:T(4,128)(2,1)} all-to-all(bf16[8,3,6144]{2,1,0:T(4,128)(2,1)} %reshape.315), channel_id=1, replica_groups=mesh['x'=4,'yl'=2,'core'=2,'z'=8,'yh'=2] {'z'}, dimensions={0} | all-to-all | bytes 589824 | tf_op jit(solution)/shard_map/all_to_all | solution.py:240
  129.5 2.0 reshape.316
  131.5 1.2 collective-permute-start.6
  132.7 1.0 constant_dynamic-update-slice_fusion.3
  133.7 2.1 collective-permute-start.7
  135.8 1.3 collective-permute-start.8
  137.1 2.5 collective-permute-done.6
  139.7 2.4 collective-permute-done.7
  142.1 4.2 %collective-permute-done.8 = bf16[24,6144]{1,0:T(8,128)(2,1)S(1)} collective-permute-done((bf16[24,6144]{1,0:T(8,128)(2,1)}, bf16[24,6144]{1,0:T(8,128)(2,1)S(1)}, u32[]{:S(2)}, u32[]{:S(2)}) %collective-permute-start.8) | collective-permute-done | bytes 294944 | tf_op jit(solution)/shard_map/ppermute | solution.py:40
  146.5 3.2 %collective-permute-start.11 = (bf16[96,6144]{1,0:T(8,128)(2,1)S(1)}, bf16[96,6144]{1,0:T(8,128)(2,1)S(1)}, u32[]{:S(2)}, u32[]{:S(2)}) collective-permute-start(bf16[96,6144]{1,0:T(8,128)(2,1)S(1)} %constant_dynamic-update-slice_fusion.refs_0_), channel_id=1, source_target_pairs={{0,33},{16,208},{32,0},{48,240},{1,32},{17,209},{33,1},{49,241},{6... | collective-permute-start | bytes 3538952 | tf_op jit(solution)/shard_map/ppermute | solution.py:40
  149.7 14.2 %collective-permute-done.9.refs_1_ = bf16[96,6144]{1,0:T(8,128)(2,1)S(1)} collective-permute-done((bf16[96,6144]{1,0:T(8,128)(2,1)S(1)}, bf16[96,6144]{1,0:T(8,128)(2,1)S(1)}, u32[]{:S(2)}, u32[]{:S(2)}) %collective-permute-start.9) | collective-permute-done | bytes 1179680 | tf_op jit(solution)/shard_map/ppermute | solution.py:40
  163.9 0.6 collective-permute-start.10
  164.9 2.5 collective-permute-start.12
  167.4 0.5 collective-permute-start.14
  167.9 6.1 %expert.2 = (bf16[96,6144]{1,0:T(8,128)(2,1)S(1)}, bf16[96,6144]{1,0:T(8,128)(2,1)S(1)}, bf16[96,6144]{1,0:T(8,128)(2,1)S(1)}) custom-call(bf16[96,6144]{1,0:T(8,128)(2,1)S(1)} %constant_dynamic-update-slice_fusion.refs_0_, bf16[96,6144]{1,0:T(8,128)(2,1)S(1)} %collective-permute-done.9.refs_1_, bf16[96,6144]{1,0:T(8,128)(2,1)S(1)} %collective-permute-done.11.refs_2_, ...), custom_call_target="tpu_custom_call" | custom-call | flops 2717908992 | bytes 16515072 | tf_op jit(solution)/shard_map/expert/pallas_call | solution.py:178
  174.0 1.0 copy-done.3
  175.1 0.4 collective-permute-start.16
  175.6 1.5 collective-permute-done.16.refs_5_
  177.1 0.8 collective-permute-done.17.refs_6_
  178.0 8.9 %expert.3 = (bf16[48,6144]{1,0:T(8,128)(2,1)S(1)}, bf16[48,6144]{1,0:T(8,128)(2,1)S(1)}, bf16[96,6144]{1,0:T(8,128)(2,1)S(1)}, bf16[96,6144]{1,0:T(8,128)(2,1)S(...) custom-call(bf16[48,6144]{1,0:T(8,128)(2,1)S(1)} %collective-permute-done.10.refs_0_, ...), custom_call_target="tpu_custom_call" | custom-call | flops 4529848320 | bytes 21233664 | tf_op jit(solution)/shard_map/expert/pallas_call | solution.py:178
  186.9 0.7 collective-permute-start.20
  187.7 0.4 collective-permute-start.21
  188.1 1.1 collective-permute-done.20
  189.3 2.4 collective-permute-done.21
  191.8 3.4 %collective-permute-start.22 = (bf16[48,6144]{1,0:T(8,128)(2,1)S(1)}, bf16[48,6144]{1,0:T(8,128)(2,1)S(1)}, u32[]{:S(2)}, u32[]{:S(2)}) collective-permute-start(bf16[48,6144]{1,0:T(8,128)(2,1)S(1)} %add_convert_fusion.4), channel_id=1, source_target_pairs={{0,33},{16,208},{32,0},{48,240},{1,32},{17,209},{33,1},{49,241},{6... | collective-permute-start | bytes 1769480 | tf_op jit(solution)/shard_map/ppermute | solution.py:40
  195.3 0.5 collective-permute-start.18
  195.8 6.9 %collective-permute-done.22 = bf16[48,6144]{1,0:T(8,128)(2,1)S(1)} collective-permute-done((bf16[48,6144]{1,0:T(8,128)(2,1)S(1)}, bf16[48,6144]{1,0:T(8,128)(2,1)S(1)}, u32[]{:S(2)}, u32[]{:S(2)}) %collective-permute-start.22) | collective-permute-done | bytes 589856 | tf_op jit(solution)/shard_map/ppermute | solution.py:40
  202.7 1.4 add_convert_fusion.2
  204.1 2.8 %collective-permute-done.24 = bf16[48,6144]{1,0:T(8,128)(2,1)S(1)} collective-permute-done((bf16[48,6144]{1,0:T(8,128)(2,1)S(1)}, bf16[48,6144]{1,0:T(8,128)(2,1)S(1)}, u32[]{:S(2)}, u32[]{:S(2)}) %collective-permute-start.24) | collective-permute-done | bytes 589856 | tf_op jit(solution)/shard_map/ppermute | solution.py:40
  206.9 1.4 add_convert_fusion.1
  208.3 3.2 %collective-permute-start.25 = (bf16[96,6144]{1,0:T(8,128)(2,1)}, bf16[96,6144]{1,0:T(8,128)(2,1)}, u32[]{:S(2)}, u32[]{:S(2)}) collective-permute-start(bf16[96,6144]{1,0:T(8,128)(2,1)} %add_convert_fusion.2), channel_id=1, source_target_pairs={{0,33},{16,208},{32,0},{48,240},{1,32},{17,209},{33,1},{49,241},{6... | collective-permute-start | bytes 3538952 | tf_op jit(solution)/shard_map/ppermute | solution.py:40
  212.0 14.0 %collective-permute-done.26 = bf16[96,6144]{1,0:T(8,128)(2,1)} collective-permute-done((bf16[96,6144]{1,0:T(8,128)(2,1)}, bf16[96,6144]{1,0:T(8,128)(2,1)}, u32[]{:S(2)}, u32[]{:S(2)}) %collective-permute-start.26) | collective-permute-done | bytes 1179680 | tf_op jit(solution)/shard_map/ppermute | solution.py:40
  226.0 2.7 %add_convert_fusion = bf16[96,6144]{1,0:T(8,128)(2,1)S(1)} fusion(bf16[96,6144]{1,0:T(8,128)(2,1)} %collective-permute-done.26, bf16[96,6144]{1,0:T(8,128)(2,1)} %collective-permute-done.25, bf16[96,6144]{1,0:T(8,128)(2,1)} %collective-permute-done.18, bf16[96,6144]{1,0:T(8,128)(2,1)S(1)} %copy-done.4), kind=kLoop, calls=%fused_computation.9 | loop fusion | flops 4718592 | bytes 5898240 | tf_op jit(solution)/shard_map/convert_element_type | solution.py:128
  228.8 1.1 collective-permute-start.29
  229.9 2.0 collective-permute-start.28
  231.9 1.3 collective-permute-start.27
  233.2 4.0 %collective-permute-done.29 = bf16[24,6144]{1,0:T(8,128)(2,1)S(1)} collective-permute-done((bf16[24,6144]{1,0:T(8,128)(2,1)S(1)}, bf16[24,6144]{1,0:T(8,128)(2,1)S(1)}, u32[]{:S(2)}, u32[]{:S(2)}) %collective-permute-start.29) | collective-permute-done | bytes 294944 | tf_op jit(solution)/shard_map/ppermute | solution.py:40
  237.2 3.1 %collective-permute-done.28 = bf16[24,6144]{1,0:T(8,128)(2,1)S(1)} collective-permute-done((bf16[24,6144]{1,0:T(8,128)(2,1)S(1)}, bf16[24,6144]{1,0:T(8,128)(2,1)S(1)}, u32[]{:S(2)}, u32[]{:S(2)}) %collective-permute-start.28) | collective-permute-done | bytes 294944 | tf_op jit(solution)/shard_map/ppermute | solution.py:40
  240.6 15.3 %all_to_all.16 = bf16[8,3,6144]{2,1,0:T(4,128)(2,1)S(1)} all-to-all(bf16[8,3,6144]{2,1,0:T(4,128)(2,1)S(1)} %reshape.317), channel_id=1, replica_groups=mesh['x'=4,'yl'=2,'core'=2,'z'=8,'yh'=2] {'z'}, dimensions={0} | all-to-all | bytes 589824 | tf_op jit(solution)/shard_map/all_to_all | solution.py:251
  256.1 0.9 fusion.1
  (81 shorter events, 4.4 us)
Async XLA Ops:
  6.5 205.0 %copy-start = (bf16[6144,8]{0,1:T(8,128)(2,1)S(1)}, bf16[6144,8]{0,1:T(8,128)(2,1)}, u32[]{:S(2)}) copy-start(bf16[6144,8]{0,1:T(8,128)(2,1)} %param.19) | copy-start | bytes 294916
  6.5 13.7 %copy-start.7 = (bf16[128,384]{1,0:T(8,128)(2,1)S(1)}, bf16[128,384]{1,0:T(8,128)(2,1)}, u32[]{:S(2)}) copy-start(bf16[128,384]{1,0:T(8,128)(2,1)} %param.12) | copy-start | bytes 294916
  6.5 46.3 %all-gather.2.cloned.1.call-start = ((), (), s32[]{:S(2)}) async-start(), calls=%async_computation.3 | async-start | bytes 5013504 | tf_op jit(solution)/shard_map/all_gather | solution.py:210
  8.7 6.4 %collective-permute-start.2 = (bf16[136,256]{1,0:T(8,128)(2,1)S(1)}, bf16[136,256]{1,0:T(8,128)(2,1)S(1)}, u32[]{:S(2)}, u32[]{:S(2)}) collective-permute-start(bf16[136,256]{1,0:T(8,128)(2,1)S(1)} %get-tuple-element.63), channel_id=1, source_target_pairs={{0,128},{64,192},{128,0},{192,64},{1,129},{65,193},{129,1},{193,65... | collective-permute-start | bytes 208904 | tf_op jit(solution)/shard_map/ppermute | solution.py:68
  11.8 4.4 %collective-permute-start.1 = (bf16[136,256]{1,0:T(8,128)(2,1)S(1)}, bf16[136,256]{1,0:T(8,128)(2,1)S(1)}, u32[]{:S(2)}, u32[]{:S(2)}) collective-permute-start(bf16[136,256]{1,0:T(8,128)(2,1)S(1)} %get-tuple-element.63), channel_id=1, source_target_pairs={{0,192},{64,0},{128,64},{192,128},{1,193},{65,1},{129,65},{193,129... | collective-permute-start | bytes 208904 | tf_op jit(solution)/shard_map/ppermute | solution.py:68
  13.0 5.5 %collective-permute-start = (bf16[136,256]{1,0:T(8,128)(2,1)S(1)}, bf16[136,256]{1,0:T(8,128)(2,1)S(1)}, u32[]{:S(2)}, u32[]{:S(2)}) collective-permute-start(bf16[136,256]{1,0:T(8,128)(2,1)S(1)} %get-tuple-element.63), channel_id=1, source_target_pairs={{0,64},{64,128},{128,192},{192,0},{1,65},{65,129},{129,193},{193,1... | collective-permute-start | bytes 208904 | tf_op jit(solution)/shard_map/ppermute | solution.py:68
  18.6 7.6 %collective-permute-start.3 = (bf16[4,136,256]{2,1,0:T(8,128)(2,1)S(1)}, bf16[4,136,256]{2,1,0:T(8,128)(2,1)S(1)}, u32[]{:S(2)}, u32[]{:S(2)}) collective-permute-start(bf16[4,136,256]{2,1,0:T(8,128)(2,1)S(1)} %get-tuple-element.61), channel_id=1, source_target_pairs={{0,32},{32,0},{1,33},{33,1},{2,34},{34,2},{3,35},{35,3},{4,36},{36... | collective-permute-start | bytes 835592 | tf_op jit(solution)/shard_map/ppermute | solution.py:24
  26.2 2.1 collective-permute-start.4
  28.4 0.7 copy-start.9
  57.4 46.7 %all-to-all-start = ((bf16[8,16,6144]{2,1,0:T(8,128)(2,1)}), bf16[8,16,6144]{2,1,0:T(8,128)(2,1)S(1)}, u32[]{:S(2)}, u32[]{:S(2)}) async-start(bf16[8,16,6144]{2,1,0:T(8,128)(2,1)} %bitcast.37), calls=%async_computation | async-start | bytes 3145728 | tf_op jit(solution)/shard_map/all_to_all | solution.py:227
  65.1 45.4 %copy-start.6 = (bf16[8,6144]{1,0:T(8,128)(2,1)S(1)}, bf16[8,6144]{1,0:T(8,128)(2,1)}, u32[]{:S(2)}) copy-start(bf16[8,6144]{1,0:T(8,128)(2,1)} %param.16) | copy-start | bytes 294916
  65.1 45.5 %copy-start.5 = (f32[6144]{0:T(1024)S(1)}, f32[6144]{0:T(1024)}, u32[]{:S(2)}) copy-start(f32[6144]{0:T(1024)} %param.18) | copy-start | bytes 73732
  104.3 6.2 %collective-permute-start.5 = (bf16[8,6144]{1,0:T(8,128)(2,1)S(1)}, bf16[8,6144]{1,0:T(8,128)(2,1)S(1)}, u32[]{:S(2)}, u32[]{:S(2)}) collective-permute-start(bf16[8,6144]{1,0:T(8,128)(2,1)S(1)} %fusion.16), channel_id=1, source_target_pairs={{0,1},{1,0},{2,3},{3,2},{4,5},{5,4},{6,7},{7,6},{8,9},{9,8},{10,11... | collective-permute-start | bytes 294920 | tf_op jit(solution)/shard_map/ppermute | solution.py:24
  111.7 56.2 %copy-start.2 = (bf16[1,6144,256]{2,1,0:T(8,128)(2,1)S(1)}, bf16[1,6144,256]{2,1,0:T(8,128)(2,1)}, u32[]{:S(2)}) copy-start(bf16[1,6144,256]{2,1,0:T(8,128)(2,1)} %param.22) | copy-start | bytes 9437188
  131.5 8.1 %collective-permute-start.6 = (bf16[24,6144]{1,0:T(8,128)(2,1)}, bf16[24,6144]{1,0:T(8,128)(2,1)S(1)}, u32[]{:S(2)}, u32[]{:S(2)}) collective-permute-start(bf16[24,6144]{1,0:T(8,128)(2,1)} %reshape.316), channel_id=1, source_target_pairs={{0,64},{16,48},{32,96},{48,17},{1,65},{17,49},{33,97},{49,16},{64,... | collective-permute-start | bytes 884744 | tf_op jit(solution)/shard_map/ppermute | solution.py:40
  133.7 8.4 %collective-permute-start.7 = (bf16[24,6144]{1,0:T(8,128)(2,1)}, bf16[24,6144]{1,0:T(8,128)(2,1)S(1)}, u32[]{:S(2)}, u32[]{:S(2)}) collective-permute-start(bf16[24,6144]{1,0:T(8,128)(2,1)} %reshape.316), channel_id=1, source_target_pairs={{0,192},{16,49},{32,224},{48,16},{1,193},{17,48},{33,225},{49,17},... | collective-permute-start | bytes 884744 | tf_op jit(solution)/shard_map/ppermute | solution.py:40
  135.8 10.5 %collective-permute-start.8 = (bf16[24,6144]{1,0:T(8,128)(2,1)}, bf16[24,6144]{1,0:T(8,128)(2,1)S(1)}, u32[]{:S(2)}, u32[]{:S(2)}) collective-permute-start(bf16[24,6144]{1,0:T(8,128)(2,1)} %reshape.316), channel_id=1, source_target_pairs={{0,128},{16,17},{32,160},{48,49},{1,129},{17,16},{33,161},{49,48},... | collective-permute-start | bytes 884744 | tf_op jit(solution)/shard_map/ppermute | solution.py:40
  142.1 25.8 %copy-start.1 = (bf16[1,6144,256]{2,1,0:T(8,128)(2,1)S(1)}, bf16[1,6144,256]{2,1,0:T(8,128)(2,1)}, u32[]{:S(2)}) copy-start(bf16[1,6144,256]{2,1,0:T(8,128)(2,1)} %param.21) | copy-start | bytes 9437188
  146.4 17.5 %collective-permute-start.9 = (bf16[96,6144]{1,0:T(8,128)(2,1)S(1)}, bf16[96,6144]{1,0:T(8,128)(2,1)S(1)}, u32[]{:S(2)}, u32[]{:S(2)}) collective-permute-start(bf16[96,6144]{1,0:T(8,128)(2,1)S(1)} %constant_dynamic-update-slice_fusion.refs_0_), channel_id=1, source_target_pairs={{0,32},{16,80},{32,1},{48,112},{1,33},{17,81},{33,0},{49,113},{64,... | collective-permute-start | bytes 3538952 | tf_op jit(solution)/shard_map/ppermute | solution.py:40
  146.5 18.4 %collective-permute-start.11 = (bf16[96,6144]{1,0:T(8,128)(2,1)S(1)}, bf16[96,6144]{1,0:T(8,128)(2,1)S(1)}, u32[]{:S(2)}, u32[]{:S(2)}) collective-permute-start(bf16[96,6144]{1,0:T(8,128)(2,1)S(1)} %constant_dynamic-update-slice_fusion.refs_0_), channel_id=1, source_target_pairs={{0,33},{16,208},{32,0},{48,240},{1,32},{17,209},{33,1},{49,241},{6... | collective-permute-start | bytes 3538952 | tf_op jit(solution)/shard_map/ppermute | solution.py:40
  163.9 11.2 %collective-permute-start.10 = (bf16[48,6144]{1,0:T(8,128)(2,1)S(1)}, bf16[48,6144]{1,0:T(8,128)(2,1)S(1)}, u32[]{:S(2)}, u32[]{:S(2)}) collective-permute-start(bf16[48,6144]{1,0:T(8,128)(2,1)S(1)} %slice.43), channel_id=1, source_target_pairs={{0,32},{16,80},{32,1},{48,112},{1,33},{17,81},{33,0},{49,113},{64,... | collective-permute-start | bytes 1769480 | tf_op jit(solution)/shard_map/ppermute | solution.py:40
  164.9 10.2 %collective-permute-start.12 = (bf16[48,6144]{1,0:T(8,128)(2,1)S(1)}, bf16[48,6144]{1,0:T(8,128)(2,1)S(1)}, u32[]{:S(2)}, u32[]{:S(2)}) collective-permute-start(bf16[48,6144]{1,0:T(8,128)(2,1)S(1)} %slice.44), channel_id=1, source_target_pairs={{0,33},{16,208},{32,0},{48,240},{1,32},{17,209},{33,1},{49,241},{6... | collective-permute-start | bytes 1769480 | tf_op jit(solution)/shard_map/ppermute | solution.py:40
  167.4 8.3 %collective-permute-start.13 = (bf16[96,6144]{1,0:T(8,128)(2,1)S(1)}, bf16[96,6144]{1,0:T(8,128)(2,1)S(1)}, u32[]{:S(2)}, u32[]{:S(2)}) collective-permute-start(bf16[96,6144]{1,0:T(8,128)(2,1)S(1)} %constant_dynamic-update-slice_fusion.refs_0_), channel_id=1, source_target_pairs={{0,16},{16,0},{1,17},{17,1},{2,18},{18,2},{3,19},{19,3},{4,20},{20... | collective-permute-start | bytes 3538952 | tf_op jit(solution)/shard_map/ppermute | solution.py:24
  167.4 10.6 %collective-permute-start.14 = (bf16[96,6144]{1,0:T(8,128)(2,1)S(1)}, bf16[96,6144]{1,0:T(8,128)(2,1)S(1)}, u32[]{:S(2)}, u32[]{:S(2)}) collective-permute-start(bf16[96,6144]{1,0:T(8,128)(2,1)S(1)} %collective-permute-done.9.refs_1_), channel_id=1, source_target_pairs={{0,16},{16,0},{1,17},{17,1},{2,18},{18,2},{3,19},{19,3},{4,20},{20... | collective-permute-start | bytes 3538952 | tf_op jit(solution)/shard_map/ppermute | solution.py:24
  167.9 10.1 %collective-permute-start.15 = (bf16[96,6144]{1,0:T(8,128)(2,1)S(1)}, bf16[96,6144]{1,0:T(8,128)(2,1)S(1)}, u32[]{:S(2)}, u32[]{:S(2)}) collective-permute-start(bf16[96,6144]{1,0:T(8,128)(2,1)S(1)} %collective-permute-done.11.refs_2_), channel_id=1, source_target_pairs={{0,16},{16,0},{1,17},{17,1},{2,18},{18,2},{3,19},{19,3},{4,20},{20... | collective-permute-start | bytes 3538952 | tf_op jit(solution)/shard_map/ppermute | solution.py:24
  174.0 1.0 copy-start.3
  175.1 2.0 collective-permute-start.16
  175.5 2.5 collective-permute-start.17
  186.9 2.3 collective-permute-start.20
  187.5 15.1 %collective-permute-start.19 = (bf16[96,6144]{1,0:T(8,128)(2,1)S(1)}, bf16[96,6144]{1,0:T(8,128)(2,1)S(1)}, u32[]{:S(2)}, u32[]{:S(2)}) collective-permute-start(bf16[96,6144]{1,0:T(8,128)(2,1)S(1)} %get-tuple-element.37), channel_id=1, source_target_pairs={{0,16},{16,0},{1,17},{17,1},{2,18},{18,2},{3,19},{19,3},{4,20},{20... | collective-permute-start | bytes 3538952 | tf_op jit(solution)/shard_map/ppermute | solution.py:24
  187.7 4.0 %collective-permute-start.21 = (bf16[48,6144]{1,0:T(8,128)(2,1)S(1)}, bf16[48,6144]{1,0:T(8,128)(2,1)S(1)}, u32[]{:S(2)}, u32[]{:S(2)}) collective-permute-start(bf16[48,6144]{1,0:T(8,128)(2,1)S(1)} %get-tuple-element.41), channel_id=1, source_target_pairs={{0,16},{16,0},{1,17},{17,1},{2,18},{18,2},{3,19},{19,3},{4,20},{20... | collective-permute-start | bytes 1769480 | tf_op jit(solution)/shard_map/ppermute | solution.py:24
  191.8 10.8 %collective-permute-start.22 = (bf16[48,6144]{1,0:T(8,128)(2,1)S(1)}, bf16[48,6144]{1,0:T(8,128)(2,1)S(1)}, u32[]{:S(2)}, u32[]{:S(2)}) collective-permute-start(bf16[48,6144]{1,0:T(8,128)(2,1)S(1)} %add_convert_fusion.4), channel_id=1, source_target_pairs={{0,33},{16,208},{32,0},{48,240},{1,32},{17,209},{33,1},{49,241},{6... | collective-permute-start | bytes 1769480 | tf_op jit(solution)/shard_map/ppermute | solution.py:40
  195.3 11.6 %collective-permute-start.23 = (bf16[96,6144]{1,0:T(8,128)(2,1)S(1)}, bf16[96,6144]{1,0:T(8,128)(2,1)S(1)}, u32[]{:S(2)}, u32[]{:S(2)}) collective-permute-start(bf16[96,6144]{1,0:T(8,128)(2,1)S(1)} %get-tuple-element.44), channel_id=1, source_target_pairs={{0,16},{16,0},{1,17},{17,1},{2,18},{18,2},{3,19},{19,3},{4,20},{20... | collective-permute-start | bytes 3538952 | tf_op jit(solution)/shard_map/ppermute | solution.py:24
  195.3 16.7 %collective-permute-start.18 = (bf16[96,6144]{1,0:T(8,128)(2,1)S(1)}, bf16[96,6144]{1,0:T(8,128)(2,1)}, u32[]{:S(2)}, u32[]{:S(2)}) collective-permute-start(bf16[96,6144]{1,0:T(8,128)(2,1)S(1)} %get-tuple-element.35), channel_id=1, source_target_pairs={{0,16},{16,0},{1,17},{17,1},{2,18},{18,2},{3,19},{19,3},{4,20},{20... | collective-permute-start | bytes 3538952 | tf_op jit(solution)/shard_map/ppermute | solution.py:24
  195.8 11.1 %collective-permute-start.24 = (bf16[48,6144]{1,0:T(8,128)(2,1)S(1)}, bf16[48,6144]{1,0:T(8,128)(2,1)S(1)}, u32[]{:S(2)}, u32[]{:S(2)}) collective-permute-start(bf16[48,6144]{1,0:T(8,128)(2,1)S(1)} %add_convert_fusion.3), channel_id=1, source_target_pairs={{0,32},{16,80},{32,1},{48,112},{1,33},{17,81},{33,0},{49,113},{64,... | collective-permute-start | bytes 1769480 | tf_op jit(solution)/shard_map/ppermute | solution.py:40
  206.9 4.9 %copy-start.8 = (s32[8,2]{0,1:T(2,128)S(1)}, s32[8,2]{0,1:T(2,128)}, u32[]{:S(2)}) copy-start(s32[8,2]{0,1:T(2,128)} %param.20) | copy-start | bytes 196
  206.9 19.1 %copy-start.4 = (bf16[96,6144]{1,0:T(8,128)(2,1)S(1)}, bf16[96,6144]{1,0:T(8,128)(2,1)}, u32[]{:S(2)}) copy-start(bf16[96,6144]{1,0:T(8,128)(2,1)} %copy-done.3) | copy-start | bytes 3538948
  208.3 17.7 %collective-permute-start.26 = (bf16[96,6144]{1,0:T(8,128)(2,1)}, bf16[96,6144]{1,0:T(8,128)(2,1)}, u32[]{:S(2)}, u32[]{:S(2)}) collective-permute-start(bf16[96,6144]{1,0:T(8,128)(2,1)} %add_convert_fusion.1), channel_id=1, source_target_pairs={{0,32},{16,80},{32,1},{48,112},{1,33},{17,81},{33,0},{49,113},{64,... | collective-permute-start | bytes 3538952 | tf_op jit(solution)/shard_map/ppermute | solution.py:40
  208.3 17.7 %collective-permute-start.25 = (bf16[96,6144]{1,0:T(8,128)(2,1)}, bf16[96,6144]{1,0:T(8,128)(2,1)}, u32[]{:S(2)}, u32[]{:S(2)}) collective-permute-start(bf16[96,6144]{1,0:T(8,128)(2,1)} %add_convert_fusion.2), channel_id=1, source_target_pairs={{0,33},{16,208},{32,0},{48,240},{1,32},{17,209},{33,1},{49,241},{6... | collective-permute-start | bytes 3538952 | tf_op jit(solution)/shard_map/ppermute | solution.py:40
  228.8 8.4 %collective-permute-start.29 = (bf16[24,6144]{1,0:T(8,128)(2,1)S(1)}, bf16[24,6144]{1,0:T(8,128)(2,1)S(1)}, u32[]{:S(2)}, u32[]{:S(2)}) collective-permute-start(bf16[24,6144]{1,0:T(8,128)(2,1)S(1)} %get-tuple-element.54), channel_id=1, source_target_pairs={{0,128},{16,17},{32,160},{48,49},{1,129},{17,16},{33,161},{49,48},... | collective-permute-start | bytes 884744 | tf_op jit(solution)/shard_map/ppermute | solution.py:40
  229.9 10.3 %collective-permute-start.28 = (bf16[24,6144]{1,0:T(8,128)(2,1)S(1)}, bf16[24,6144]{1,0:T(8,128)(2,1)S(1)}, u32[]{:S(2)}, u32[]{:S(2)}) collective-permute-start(bf16[24,6144]{1,0:T(8,128)(2,1)S(1)} %get-tuple-element.55), channel_id=1, source_target_pairs={{0,64},{16,48},{32,96},{48,17},{1,65},{17,49},{33,97},{49,16},{64,... | collective-permute-start | bytes 884744 | tf_op jit(solution)/shard_map/ppermute | solution.py:40
  231.9 8.4 %collective-permute-start.27 = (bf16[24,6144]{1,0:T(8,128)(2,1)S(1)}, bf16[24,6144]{1,0:T(8,128)(2,1)S(1)}, u32[]{:S(2)}, u32[]{:S(2)}) collective-permute-start(bf16[24,6144]{1,0:T(8,128)(2,1)S(1)} %get-tuple-element.53), channel_id=1, source_target_pairs={{0,192},{16,49},{32,224},{48,16},{1,193},{17,48},{33,225},{49,17},... | collective-permute-start | bytes 884744 | tf_op jit(solution)/shard_map/ppermute | solution.py:40
Sparse Core Ops, SparseCore 0:
  9.2 43.6 all-gather.1

commit v2 on v0

--- a/solution.py
+++ b/solution.py
@@ -115,9 +115,9 @@
     far_first, far_second = lax.optimization_barrier((far_first, far_second))
     half = far_first.shape[0]
     far_first, far_second = plane_shift(far_first, -1, 1), plane_shift(far_second, 1, 1)
-    left, right = [total(mine[i], swap(other[i], "core")) for i in (1, 2)]
-    left = jnp.concatenate([left[:half] + far_first.astype(F32), left[half:]]).astype(BF)
-    right = jnp.concatenate([right[:half], right[half:] + far_second.astype(F32)]).astype(BF)
+    left = total(mine[1], swap(other[1], "core"), jnp.pad(far_first, ((0, half), (0, 0))))
+    right = total(mine[2], swap(other[2], "core"), jnp.pad(far_second, ((half, 0), (0, 0))))
+    left, right = left.astype(BF), right.astype(BF)
     left, right = lax.optimization_barrier((left, right))
     left, right = plane_shift(left, -1, 1), plane_shift(right, 1, 1)
     rows = total(mine[0], swap(other[0], "core"), left, right).astype(BF)
@@ -178,7 +178,7 @@
         out_specs=[pl.BlockSpec((b.shape[0], wide), lambda i: (0, trail(i))) for b in blocks],
         out_shape=[jax.ShapeDtypeStruct(b.shape, BF) for b in blocks],
         scratch_shapes=[pltpu.VMEM((rows, 2 * units), F32), pltpu.VMEM((rows, units), BF)],
-        compiler_params=pltpu.CompilerParams(vmem_limit_bytes=40 * 1024 * 1024),
+        compiler_params=pltpu.CompilerParams(vmem_limit_bytes=28 * 1024 * 1024),
         cost_estimate=pl.CostEstimate(
             flops=6 * rows * features * units,
             bytes_accessed=2 * (3 * features * units + 2 * rows * features),

time: 258 us -> 262 us (1.016)
  local copies, waits for them, and re-layouts: 4.52 us -> 10.9 us
  Pallas kernels: 15 us -> 11.8 us
    pallas_call x2, Pallas kernels: 15 us -> 11.8 us  [expert(): pl.pallas_call(functools.partial(expert_kernel, len(blocks)), grid=(2 * S...]
    unnamed x19 -> x29, local copies, waits for them, and re-layouts: 1.97 us -> 4.86 us
    convert_element_type x0 -> x2, other arithmetic: none -> 2.79 us  [scatter_plane(): left, right = (left.astype(BF), right.astype(BF))]
  transfers between devices with their start and end apart: 30 -> 30, of which waited for: 19 -> 17; matrix products, arithmetic and copies ran while one was open for 5% -> 5% of each run, Pallas kernels for 3% -> 2%
where the time goes in v2:
time: 262 us; the launch traced here: 261 us
  waiting for transfers between devices  98.8 us (38%)
  blocking collectives  81.5 us (31%)
  starting transfers between devices  26.4 us (10%)
  between operations  13.7 us (5%)
  Pallas kernels  11.8 us (5%)
  local copies, waits for them, and re-layouts  10.9 us (4%)
  other arithmetic  8.97 us (3%)
  matrix products  8.52 us (3%)
    ppermute x14, waiting for transfers between devices, plane_shift(): return lax.ppermute(value, PLANE, pairs)  64 us
    all_to_all x1, blocking collectives, shards(): lax.all_to_all(head_partial.reshape(16, tokens, width), EXP, split_axis=0...  48.6 us
    all_gather x1, waiting for transfers between devices, shards(): w_out_all = lax.all_gather(w_out, CTX, axis=1, tiled=True)  20.8 us
    all_to_all x1, blocking collectives, shards(): lax.all_to_all(outgoing.reshape(EXPERTS, SLOTS, width), 'z', split_axis=0...  19.1 us
    ppermute x14, starting transfers between devices, plane_shift(): return lax.ppermute(value, PLANE, pairs)  17.3 us
    all_to_all x1, blocking collectives, shards(): lax.all_to_all(slot_sums.reshape(EXPERTS, SLOTS, width), 'z', split_axis=...  13.8 us
    pallas_call x2, Pallas kernels, expert(): pl.pallas_call(functools.partial(expert_kernel, len(blocks)), grid=(2 * S...  11.8 us
    ppermute x12, waiting for transfers between devices, swap(): return lax.ppermute(value, axis, [(0, 1), (1, 0)])  10.5 us
  transfers between devices with their start and end apart: 30, of which 17 were waited for; matrix products, arithmetic and copies ran while one was open for 5% of the time, Pallas kernels for 2%

profile of v2, /device:TPU:32, one launch (start us, length us, event | category | flops | bytes accessed | tf_op | source)
XLA Modules:
  0.0 260.7 jit_solution(12078157021457983309)
XLA Ops:
  6.5 0.7 all-gather.2.cloned.1.call-update
  7.3 0.8 constant_dynamic-slice_fusion
  8.1 0.7 convert_bitcast_fusion
  8.7 2.8 %collective-permute-start.1 = (bf16[136,256]{1,0:T(8,128)(2,1)S(1)}, bf16[136,256]{1,0:T(8,128)(2,1)S(1)}, u32[]{:S(2)}, u32[]{:S(2)}) collective-permute-start(bf16[136,256]{1,0:T(8,128)(2,1)S(1)} %get-tuple-element.53), channel_id=1, source_target_pairs={{0,192},{64,0},{128,64},{192,128},{1,193},{65,1},{129,65},{193,129... | collective-permute-start | bytes 208904 | tf_op jit(solution)/shard_map/ppermute | solution.py:68
  11.6 2.3 collective-permute-start.2
  13.9 0.8 copy.30
  15.1 2.9 %collective-permute-done = bf16[136,256]{1,0:T(8,128)(2,1)S(1)} collective-permute-done((bf16[136,256]{1,0:T(8,128)(2,1)S(1)}, bf16[136,256]{1,0:T(8,128)(2,1)S(1)}, u32[]{:S(2)}, u32[]{:S(2)}) %collective-permute-start) | collective-permute-done | bytes 69664 | tf_op jit(solution)/shard_map/ppermute | solution.py:68
  18.0 1.7 collective-permute-start.3
  20.1 5.3 %collective-permute-done.3 = bf16[4,136,256]{2,1,0:T(8,128)(2,1)S(1)} collective-permute-done((bf16[4,136,256]{2,1,0:T(8,128)(2,1)S(1)}, bf16[4,136,256]{2,1,0:T(8,128)(2,1)S(1)}, u32[]{:S(2)}, u32[]{:S(2)}) %collective-permute-start.3) | collective-permute-done | bytes 278560 | tf_op jit(solution)/shard_map/ppermute | solution.py:24
  25.6 1.8 collective-permute-done.4
  27.6 0.3 fusion.33
  27.9 0.3 copy-done.11
  28.2 1.3 compare_and_fusion
  29.5 1.6 fusion.34
  31.1 1.5 fusion.11
  32.6 20.8 %all-gather.2.cloned.1.call-done = bf16[384,6144]{1,0:T(8,128)(2,1)} async-done(((bf16[384,384]{1,0:T(8,128)(2,1)}), bf16[384,6144]{1,0:T(8,128)(2,1)}) %all-gather.2.cloned.1.call-update) | async-done | bytes 4718608 | tf_op jit(solution)/shard_map/all_gather | solution.py:205
  53.4 3.4 %convolution_convert_fusion = bf16[128,6144]{1,0:T(8,128)(2,1)S(1)} fusion(bf16[128,384]{0,1:T(8,128)(2,1)S(1)} %bitcast.92, bf16[384,6144]{1,0:T(8,128)(2,1)} %all-gather.2.cloned.1.call-done), kind=kOutput, calls=%fused_computation.1 | convolution fusion | flops 604766208 | bytes 6389760 | tf_op jit(solution)/shard_map/dot_general | solution.py:207
  56.8 48.6 %all_to_all.15 = bf16[16,8,6144]{2,1,0:T(8,128)(2,1)S(1)} all-to-all(bf16[16,8,6144]{2,1,0:T(8,128)(2,1)S(1)} %bitcast.84), channel_id=1, replica_groups=mesh['x'=4,'yl'=2,'core'=2,'z'=8,'yh'=2] {'z','yh'}, dimensions={0} | all-to-all | bytes 3145728 | tf_op jit(solution)/shard_map/all_to_all | solution.py:221
  105.4 0.2 convert_reduce_fusion
  105.6 0.7 copy-done.6
  106.5 1.0 convolution_convert_fusion.1
  107.5 2.0 reshape.310
  109.6 19.1 %all_to_all.16 = bf16[8,3,6144]{2,1,0:T(4,128)(2,1)} all-to-all(bf16[8,3,6144]{2,1,0:T(4,128)(2,1)} %reshape.310), channel_id=1, replica_groups=mesh['x'=4,'yl'=2,'core'=2,'z'=8,'yh'=2] {'z'}, dimensions={0} | all-to-all | bytes 589824 | tf_op jit(solution)/shard_map/all_to_all | solution.py:231
  128.7 2.0 reshape.311
  130.7 2.5 collective-permute-start.7
  133.2 1.7 collective-permute-start.6
  134.9 0.3 collective-permute-start.5
  135.2 1.0 constant_dynamic-update-slice_fusion.3
  136.2 7.0 %collective-permute-done.5 = bf16[24,6144]{1,0:T(8,128)(2,1)S(1)} collective-permute-done((bf16[24,6144]{1,0:T(8,128)(2,1)}, bf16[24,6144]{1,0:T(8,128)(2,1)S(1)}, u32[]{:S(2)}, u32[]{:S(2)}) %collective-permute-start.5) | collective-permute-done | bytes 294944 | tf_op jit(solution)/shard_map/ppermute | solution.py:40
  143.4 0.3 collective-permute-start.9
  143.6 2.0 collective-permute-start.8
  145.7 14.2 %collective-permute-done.9.refs_2_ = bf16[96,6144]{1,0:T(8,128)(2,1)S(1)} collective-permute-done((bf16[96,6144]{1,0:T(8,128)(2,1)S(1)}, bf16[96,6144]{1,0:T(8,128)(2,1)S(1)}, u32[]{:S(2)}, u32[]{:S(2)}) %collective-permute-start.9) | collective-permute-done | bytes 1179680 | tf_op jit(solution)/shard_map/ppermute | solution.py:40
  159.9 1.3 collective-permute-start.11
  161.2 0.9 collective-permute-start.10
  162.1 0.5 collective-permute-start.13
  162.6 7.2 %collective-permute-done.11.refs_4_ = bf16[48,6144]{1,0:T(8,128)(2,1)S(1)} collective-permute-done((bf16[48,6144]{1,0:T(8,128)(2,1)S(1)}, bf16[48,6144]{1,0:T(8,128)(2,1)S(1)}, u32[]{:S(2)}, u32[]{:S(2)}) %collective-permute-start.11) | collective-permute-done | bytes 589856 | tf_op jit(solution)/shard_map/ppermute | solution.py:40
  169.8 2.5 collective-permute-done.10.refs_3_
  172.4 2.0 collective-permute-done.15.refs_3_
  174.4 1.9 copy-done.3
  176.3 6.2 %expert.3 = (bf16[96,6144]{1,0:T(8,128)(2,1)}, bf16[96,6144]{1,0:T(8,128)(2,1)S(1)}, bf16[96,6144]{1,0:T(8,128)(2,1)S(1)}, bf16[48,6144]{1,0:T(8,128)(2,1)S(1)}, bf16[48,6144]{1,0:T(8,128)(2,1)S(1)}) custom-call(bf16[96,6144]{1,0:T(8,128)(2,1)S(1)} %collective-permute-done.12.refs_0_, bf16[96,6144]{1,0:T(8,128)(2,1)S(1)} %collective-permute-done.13.refs_1_, ...), custom_call_target="tpu_custom_call" | custom-call | flops 3623878656 | bytes 18874368 | tf_op jit(solution)/shard_map/expert/pallas_call | solution.py:173
  182.7 5.6 %expert.2 = (bf16[96,6144]{1,0:T(8,128)(2,1)S(1)}, bf16[96,6144]{1,0:T(8,128)(2,1)S(1)}, bf16[96,6144]{1,0:T(8,128)(2,1)S(1)}, bf16[48,6144]{1,0:T(8,128)(2,1)S(1)}, bf16[48,6144]{1,0:T(8,128)(2,1)S(1)}) custom-call(bf16[96,6144]{1,0:T(8,128)(2,1)S(1)} %constant_dynamic-update-slice_fusion.refs_0_, bf16[96,6144]{1,0:T(8,128)(2,1)S(1)} %collective-permute-done.8.refs_1_, ...), custom_call_target="tpu_custom_call" | custom-call | flops 3623878656 | bytes 18874368 | tf_op jit(solution)/shard_map/expert/pallas_call | solution.py:173
  188.3 0.5 collective-permute-start.20
  189.0 1.4 collective-permute-done.20
  190.5 0.8 collective-permute-start.21
  191.3 0.9 collective-permute-start.17
  192.3 0.9 collective-permute-start.23
  193.2 7.3 %collective-permute-done.21 = bf16[48,6144]{1,0:T(8,128)(2,1)S(1)} collective-permute-done((bf16[48,6144]{1,0:T(8,128)(2,1)S(1)}, bf16[48,6144]{1,0:T(8,128)(2,1)S(1)}, u32[]{:S(2)}, u32[]{:S(2)}) %collective-permute-start.21) | collective-permute-done | bytes 589856 | tf_op jit(solution)/shard_map/ppermute | solution.py:40
  200.5 1.4 add_convert_fusion.2
  201.9 1.5 collective-permute-done.23
  203.4 1.4 add_convert_fusion.1
  204.8 0.5 collective-permute-start.24
  205.2 1.6 collective-permute-start.25
  207.2 14.1 %collective-permute-done.24 = bf16[96,6144]{1,0:T(8,128)(2,1)} collective-permute-done((bf16[96,6144]{1,0:T(8,128)(2,1)}, bf16[96,6144]{1,0:T(8,128)(2,1)}, u32[]{:S(2)}, u32[]{:S(2)}) %collective-permute-start.24) | collective-permute-done | bytes 1179680 | tf_op jit(solution)/shard_map/ppermute | solution.py:40
  221.3 1.7 collective-permute-done.25
  223.0 2.3 add_convert_fusion
  225.4 1.7 collective-permute-start.26
  227.1 2.2 collective-permute-start.28
  229.3 0.7 collective-permute-start.27
  230.1 2.1 collective-permute-done.26
  232.2 3.2 %collective-permute-done.28 = bf16[24,6144]{1,0:T(8,128)(2,1)S(1)} collective-permute-done((bf16[24,6144]{1,0:T(8,128)(2,1)S(1)}, bf16[24,6144]{1,0:T(8,128)(2,1)S(1)}, u32[]{:S(2)}, u32[]{:S(2)}) %collective-permute-start.28) | collective-permute-done | bytes 294944 | tf_op jit(solution)/shard_map/ppermute | solution.py:40
  235.4 3.1 %collective-permute-done.27 = bf16[24,6144]{1,0:T(8,128)(2,1)S(1)} collective-permute-done((bf16[24,6144]{1,0:T(8,128)(2,1)S(1)}, bf16[24,6144]{1,0:T(8,128)(2,1)S(1)}, u32[]{:S(2)}, u32[]{:S(2)}) %collective-permute-start.27) | collective-permute-done | bytes 294944 | tf_op jit(solution)/shard_map/ppermute | solution.py:40
  238.8 13.8 %all_to_all.17 = bf16[8,3,6144]{2,1,0:T(4,128)(2,1)S(1)} all-to-all(bf16[8,3,6144]{2,1,0:T(4,128)(2,1)S(1)} %reshape.312), channel_id=1, replica_groups=mesh['x'=4,'yl'=2,'core'=2,'z'=8,'yh'=2] {'z'}, dimensions={0} | all-to-all | bytes 589824 | tf_op jit(solution)/shard_map/all_to_all | solution.py:242
  252.6 0.3 reshape.313
  252.9 0.9 fusion.1
  (82 shorter events, 3.2 us)
Async XLA Ops:
  6.5 200.3 %copy-start = (bf16[6144,8]{0,1:T(8,128)(2,1)S(1)}, bf16[6144,8]{0,1:T(8,128)(2,1)}, u32[]{:S(2)}) copy-start(bf16[6144,8]{0,1:T(8,128)(2,1)} %param.19) | copy-start | bytes 294916
  6.5 13.3 %copy-start.8 = (bf16[128,384]{1,0:T(8,128)(2,1)S(1)}, bf16[128,384]{1,0:T(8,128)(2,1)}, u32[]{:S(2)}) copy-start(bf16[128,384]{1,0:T(8,128)(2,1)} %param.12) | copy-start | bytes 294916
  6.5 46.9 %all-gather.2.cloned.1.call-start = ((), (), s32[]{:S(2)}) async-start(), calls=%async_computation.3 | async-start | bytes 5013504 | tf_op jit(solution)/shard_map/all_gather | solution.py:205
  8.7 6.3 %collective-permute-start.1 = (bf16[136,256]{1,0:T(8,128)(2,1)S(1)}, bf16[136,256]{1,0:T(8,128)(2,1)S(1)}, u32[]{:S(2)}, u32[]{:S(2)}) collective-permute-start(bf16[136,256]{1,0:T(8,128)(2,1)S(1)} %get-tuple-element.53), channel_id=1, source_target_pairs={{0,192},{64,0},{128,64},{192,128},{1,193},{65,1},{129,65},{193,129... | collective-permute-start | bytes 208904 | tf_op jit(solution)/shard_map/ppermute | solution.py:68
  11.6 6.4 %collective-permute-start = (bf16[136,256]{1,0:T(8,128)(2,1)S(1)}, bf16[136,256]{1,0:T(8,128)(2,1)S(1)}, u32[]{:S(2)}, u32[]{:S(2)}) collective-permute-start(bf16[136,256]{1,0:T(8,128)(2,1)S(1)} %get-tuple-element.53), channel_id=1, source_target_pairs={{0,64},{64,128},{128,192},{192,0},{1,65},{65,129},{129,193},{193,1... | collective-permute-start | bytes 208904 | tf_op jit(solution)/shard_map/ppermute | solution.py:68
  11.6 6.4 %collective-permute-start.2 = (bf16[136,256]{1,0:T(8,128)(2,1)S(1)}, bf16[136,256]{1,0:T(8,128)(2,1)S(1)}, u32[]{:S(2)}, u32[]{:S(2)}) collective-permute-start(bf16[136,256]{1,0:T(8,128)(2,1)S(1)} %get-tuple-element.53), channel_id=1, source_target_pairs={{0,128},{64,192},{128,0},{192,64},{1,129},{65,193},{129,1},{193,65... | collective-permute-start | bytes 208904 | tf_op jit(solution)/shard_map/ppermute | solution.py:68
  18.0 7.3 %collective-permute-start.3 = (bf16[4,136,256]{2,1,0:T(8,128)(2,1)S(1)}, bf16[4,136,256]{2,1,0:T(8,128)(2,1)S(1)}, u32[]{:S(2)}, u32[]{:S(2)}) collective-permute-start(bf16[4,136,256]{2,1,0:T(8,128)(2,1)S(1)} %get-tuple-element.51), channel_id=1, source_target_pairs={{0,32},{32,0},{1,33},{33,1},{2,34},{34,2},{3,35},{35,3},{4,36},{36... | collective-permute-start | bytes 835592 | tf_op jit(solution)/shard_map/ppermute | solution.py:24
  25.4 2.0 collective-permute-start.4
  27.6 0.7 copy-start.11
  105.4 0.9 copy-start.6
  105.4 1.1 copy-start.9
  107.5 66.9 %copy-start.2 = (bf16[1,6144,256]{2,1,0:T(8,128)(2,1)S(1)}, bf16[1,6144,256]{2,1,0:T(8,128)(2,1)}, u32[]{:S(2)}) copy-start(bf16[1,6144,256]{2,1,0:T(8,128)(2,1)} %param.22) | copy-start | bytes 9437188
  130.7 12.7 %collective-permute-start.7 = (bf16[24,6144]{1,0:T(8,128)(2,1)}, bf16[24,6144]{1,0:T(8,128)(2,1)S(1)}, u32[]{:S(2)}, u32[]{:S(2)}) collective-permute-start(bf16[24,6144]{1,0:T(8,128)(2,1)} %reshape.311), channel_id=1, source_target_pairs={{0,128},{16,17},{32,160},{48,49},{1,129},{17,16},{33,161},{49,48},... | collective-permute-start | bytes 884744 | tf_op jit(solution)/shard_map/ppermute | solution.py:40
  133.2 10.1 %collective-permute-start.6 = (bf16[24,6144]{1,0:T(8,128)(2,1)}, bf16[24,6144]{1,0:T(8,128)(2,1)S(1)}, u32[]{:S(2)}, u32[]{:S(2)}) collective-permute-start(bf16[24,6144]{1,0:T(8,128)(2,1)} %reshape.311), channel_id=1, source_target_pairs={{0,192},{16,49},{32,224},{48,16},{1,193},{17,48},{33,225},{49,17},... | collective-permute-start | bytes 884744 | tf_op jit(solution)/shard_map/ppermute | solution.py:40
  134.9 8.4 %collective-permute-start.5 = (bf16[24,6144]{1,0:T(8,128)(2,1)}, bf16[24,6144]{1,0:T(8,128)(2,1)S(1)}, u32[]{:S(2)}, u32[]{:S(2)}) collective-permute-start(bf16[24,6144]{1,0:T(8,128)(2,1)} %reshape.311), channel_id=1, source_target_pairs={{0,64},{16,48},{32,96},{48,17},{1,65},{17,49},{33,97},{49,16},{64,... | collective-permute-start | bytes 884744 | tf_op jit(solution)/shard_map/ppermute | solution.py:40
  143.3 31.1 %copy-start.1 = (bf16[1,6144,256]{2,1,0:T(8,128)(2,1)S(1)}, bf16[1,6144,256]{2,1,0:T(8,128)(2,1)}, u32[]{:S(2)}) copy-start(bf16[1,6144,256]{2,1,0:T(8,128)(2,1)} %param.21) | copy-start | bytes 9437188
  143.4 16.5 %collective-permute-start.9 = (bf16[96,6144]{1,0:T(8,128)(2,1)S(1)}, bf16[96,6144]{1,0:T(8,128)(2,1)S(1)}, u32[]{:S(2)}, u32[]{:S(2)}) collective-permute-start(bf16[96,6144]{1,0:T(8,128)(2,1)S(1)} %constant_dynamic-update-slice_fusion.refs_0_), channel_id=1, source_target_pairs={{0,33},{16,208},{32,0},{48,240},{1,32},{17,209},{33,1},{49,241},{6... | collective-permute-start | bytes 3538952 | tf_op jit(solution)/shard_map/ppermute | solution.py:40
  143.6 17.5 %collective-permute-start.8 = (bf16[96,6144]{1,0:T(8,128)(2,1)S(1)}, bf16[96,6144]{1,0:T(8,128)(2,1)S(1)}, u32[]{:S(2)}, u32[]{:S(2)}) collective-permute-start(bf16[96,6144]{1,0:T(8,128)(2,1)S(1)} %constant_dynamic-update-slice_fusion.refs_0_), channel_id=1, source_target_pairs={{0,32},{16,80},{32,1},{48,112},{1,33},{17,81},{33,0},{49,113},{64,... | collective-permute-start | bytes 3538952 | tf_op jit(solution)/shard_map/ppermute | solution.py:40
  145.7 26.7 %collective-permute-start.12 = (bf16[96,6144]{1,0:T(8,128)(2,1)S(1)}, bf16[96,6144]{1,0:T(8,128)(2,1)S(1)}, u32[]{:S(2)}, u32[]{:S(2)}) collective-permute-start(bf16[96,6144]{1,0:T(8,128)(2,1)S(1)} %constant_dynamic-update-slice_fusion.refs_0_), channel_id=1, source_target_pairs={{0,16},{16,0},{1,17},{17,1},{2,18},{18,2},{3,19},{19,3},{4,20},{20... | collective-permute-start | bytes 3538952 | tf_op jit(solution)/shard_map/ppermute | solution.py:24
  159.9 10.0 %collective-permute-start.11 = (bf16[48,6144]{1,0:T(8,128)(2,1)S(1)}, bf16[48,6144]{1,0:T(8,128)(2,1)S(1)}, u32[]{:S(2)}, u32[]{:S(2)}) collective-permute-start(bf16[48,6144]{1,0:T(8,128)(2,1)S(1)} %slice.44), channel_id=1, source_target_pairs={{0,33},{16,208},{32,0},{48,240},{1,32},{17,209},{33,1},{49,241},{6... | collective-permute-start | bytes 1769480 | tf_op jit(solution)/shard_map/ppermute | solution.py:40
  161.2 11.2 %collective-permute-start.10 = (bf16[48,6144]{1,0:T(8,128)(2,1)S(1)}, bf16[48,6144]{1,0:T(8,128)(2,1)S(1)}, u32[]{:S(2)}, u32[]{:S(2)}) collective-permute-start(bf16[48,6144]{1,0:T(8,128)(2,1)S(1)} %slice.43), channel_id=1, source_target_pairs={{0,32},{16,80},{32,1},{48,112},{1,33},{17,81},{33,0},{49,113},{64,... | collective-permute-start | bytes 1769480 | tf_op jit(solution)/shard_map/ppermute | solution.py:40
  162.1 12.3 %collective-permute-start.14 = (bf16[96,6144]{1,0:T(8,128)(2,1)S(1)}, bf16[96,6144]{1,0:T(8,128)(2,1)S(1)}, u32[]{:S(2)}, u32[]{:S(2)}) collective-permute-start(bf16[96,6144]{1,0:T(8,128)(2,1)S(1)} %collective-permute-done.9.refs_2_), channel_id=1, source_target_pairs={{0,16},{16,0},{1,17},{17,1},{2,18},{18,2},{3,19},{19,3},{4,20},{20... | collective-permute-start | bytes 3538952 | tf_op jit(solution)/shard_map/ppermute | solution.py:24
  162.1 12.3 %collective-permute-start.13 = (bf16[96,6144]{1,0:T(8,128)(2,1)S(1)}, bf16[96,6144]{1,0:T(8,128)(2,1)S(1)}, u32[]{:S(2)}, u32[]{:S(2)}) collective-permute-start(bf16[96,6144]{1,0:T(8,128)(2,1)S(1)} %collective-permute-done.8.refs_1_), channel_id=1, source_target_pairs={{0,16},{16,0},{1,17},{17,1},{2,18},{18,2},{3,19},{19,3},{4,20},{20... | collective-permute-start | bytes 3538952 | tf_op jit(solution)/shard_map/ppermute | solution.py:24
  169.8 2.6 collective-permute-start.16
  172.4 2.0 collective-permute-start.15
  174.4 1.9 copy-start.3
  182.5 6.4 %collective-permute-start.19 = (bf16[48,6144]{1,0:T(8,128)(2,1)S(1)}, bf16[48,6144]{1,0:T(8,128)(2,1)S(1)}, u32[]{:S(2)}, u32[]{:S(2)}) collective-permute-start(bf16[48,6144]{1,0:T(8,128)(2,1)S(1)} %get-tuple-element.31), channel_id=1, source_target_pairs={{0,16},{16,0},{1,17},{17,1},{2,18},{18,2},{3,19},{19,3},{4,20},{20... | collective-permute-start | bytes 1769480 | tf_op jit(solution)/shard_map/ppermute | solution.py:24
  188.3 2.2 copy-start.4
  188.3 2.1 collective-permute-start.20
  188.8 11.7 %collective-permute-start.18 = (bf16[96,6144]{1,0:T(8,128)(2,1)S(1)}, bf16[96,6144]{1,0:T(8,128)(2,1)S(1)}, u32[]{:S(2)}, u32[]{:S(2)}) collective-permute-start(bf16[96,6144]{1,0:T(8,128)(2,1)S(1)} %get-tuple-element.29), channel_id=1, source_target_pairs={{0,16},{16,0},{1,17},{17,1},{2,18},{18,2},{3,19},{19,3},{4,20},{20... | collective-permute-start | bytes 3538952 | tf_op jit(solution)/shard_map/ppermute | solution.py:24
  190.5 10.0 %collective-permute-start.21 = (bf16[48,6144]{1,0:T(8,128)(2,1)S(1)}, bf16[48,6144]{1,0:T(8,128)(2,1)S(1)}, u32[]{:S(2)}, u32[]{:S(2)}) collective-permute-start(bf16[48,6144]{1,0:T(8,128)(2,1)S(1)} %add_convert_fusion.4), channel_id=1, source_target_pairs={{0,33},{16,208},{32,0},{48,240},{1,32},{17,209},{33,1},{49,241},{6... | collective-permute-start | bytes 1769480 | tf_op jit(solution)/shard_map/ppermute | solution.py:40
  191.3 15.8 %collective-permute-start.17 = (bf16[96,6144]{1,0:T(8,128)(2,1)}, bf16[96,6144]{1,0:T(8,128)(2,1)S(1)}, u32[]{:S(2)}, u32[]{:S(2)}) collective-permute-start(bf16[96,6144]{1,0:T(8,128)(2,1)} %get-tuple-element.27), channel_id=1, source_target_pairs={{0,16},{16,0},{1,17},{17,1},{2,18},{18,2},{3,19},{19,3},{4,20},{20... | collective-permute-start | bytes 3538952 | tf_op jit(solution)/shard_map/ppermute | solution.py:24
  192.3 11.1 %collective-permute-start.22 = (bf16[96,6144]{1,0:T(8,128)(2,1)S(1)}, bf16[96,6144]{1,0:T(8,128)(2,1)S(1)}, u32[]{:S(2)}, u32[]{:S(2)}) collective-permute-start(bf16[96,6144]{1,0:T(8,128)(2,1)S(1)} %get-tuple-element.36), channel_id=1, source_target_pairs={{0,16},{16,0},{1,17},{17,1},{2,18},{18,2},{3,19},{19,3},{4,20},{20... | collective-permute-start | bytes 3538952 | tf_op jit(solution)/shard_map/ppermute | solution.py:24
  192.3 11.1 %collective-permute-start.23 = (bf16[48,6144]{1,0:T(8,128)(2,1)S(1)}, bf16[48,6144]{1,0:T(8,128)(2,1)S(1)}, u32[]{:S(2)}, u32[]{:S(2)}) collective-permute-start(bf16[48,6144]{1,0:T(8,128)(2,1)S(1)} %add_convert_fusion.3), channel_id=1, source_target_pairs={{0,32},{16,80},{32,1},{48,112},{1,33},{17,81},{33,0},{49,113},{64,... | collective-permute-start | bytes 1769480 | tf_op jit(solution)/shard_map/ppermute | solution.py:40
  203.4 3.6 %copy-start.10 = (s32[8,2]{0,1:T(2,128)S(1)}, s32[8,2]{0,1:T(2,128)}, u32[]{:S(2)}) copy-start(s32[8,2]{0,1:T(2,128)} %param.20) | copy-start | bytes 196
  203.4 19.6 %copy-start.5 = (bf16[96,6144]{1,0:T(8,128)(2,1)S(1)}, bf16[96,6144]{1,0:T(8,128)(2,1)}, u32[]{:S(2)}) copy-start(bf16[96,6144]{1,0:T(8,128)(2,1)} %copy-done.4) | copy-start | bytes 3538948
  204.8 16.5 %collective-permute-start.24 = (bf16[96,6144]{1,0:T(8,128)(2,1)}, bf16[96,6144]{1,0:T(8,128)(2,1)}, u32[]{:S(2)}, u32[]{:S(2)}) collective-permute-start(bf16[96,6144]{1,0:T(8,128)(2,1)} %add_convert_fusion.2), channel_id=1, source_target_pairs={{0,33},{16,208},{32,0},{48,240},{1,32},{17,209},{33,1},{49,241},{6... | collective-permute-start | bytes 3538952 | tf_op jit(solution)/shard_map/ppermute | solution.py:40
  205.2 17.7 %collective-permute-start.25 = (bf16[96,6144]{1,0:T(8,128)(2,1)}, bf16[96,6144]{1,0:T(8,128)(2,1)}, u32[]{:S(2)}, u32[]{:S(2)}) collective-permute-start(bf16[96,6144]{1,0:T(8,128)(2,1)} %add_convert_fusion.1), channel_id=1, source_target_pairs={{0,32},{16,80},{32,1},{48,112},{1,33},{17,81},{33,0},{49,113},{64,... | collective-permute-start | bytes 3538952 | tf_op jit(solution)/shard_map/ppermute | solution.py:40
  225.4 6.8 %collective-permute-start.26 = (bf16[24,6144]{1,0:T(8,128)(2,1)S(1)}, bf16[24,6144]{1,0:T(8,128)(2,1)S(1)}, u32[]{:S(2)}, u32[]{:S(2)}) collective-permute-start(bf16[24,6144]{1,0:T(8,128)(2,1)S(1)} %get-tuple-element.43), channel_id=1, source_target_pairs={{0,192},{16,49},{32,224},{48,16},{1,193},{17,48},{33,225},{49,17},... | collective-permute-start | bytes 884744 | tf_op jit(solution)/shard_map/ppermute | solution.py:40
  227.1 8.3 %collective-permute-start.28 = (bf16[24,6144]{1,0:T(8,128)(2,1)S(1)}, bf16[24,6144]{1,0:T(8,128)(2,1)S(1)}, u32[]{:S(2)}, u32[]{:S(2)}) collective-permute-start(bf16[24,6144]{1,0:T(8,128)(2,1)S(1)} %get-tuple-element.44), channel_id=1, source_target_pairs={{0,128},{16,17},{32,160},{48,49},{1,129},{17,16},{33,161},{49,48},... | collective-permute-start | bytes 884744 | tf_op jit(solution)/shard_map/ppermute | solution.py:40
  229.3 9.1 %collective-permute-start.27 = (bf16[24,6144]{1,0:T(8,128)(2,1)S(1)}, bf16[24,6144]{1,0:T(8,128)(2,1)S(1)}, u32[]{:S(2)}, u32[]{:S(2)}) collective-permute-start(bf16[24,6144]{1,0:T(8,128)(2,1)S(1)} %get-tuple-element.45), channel_id=1, source_target_pairs={{0,64},{16,48},{32,96},{48,17},{1,65},{17,49},{33,97},{49,16},{64,... | collective-permute-start | bytes 884744 | tf_op jit(solution)/shard_map/ppermute | solution.py:40
  238.6 14.3 %copy-start.7 = (bf16[8,6144]{1,0:T(8,128)(2,1)S(1)}, bf16[8,6144]{1,0:T(8,128)(2,1)}, u32[]{:S(2)}) copy-start(bf16[8,6144]{1,0:T(8,128)(2,1)} %param.16) | copy-start | bytes 294916
Sparse Core Ops, SparseCore 0:
  9.2 44.1 all-gather.1

commit v3 on v0

--- a/solution.py
+++ b/solution.py
@@ -99,15 +99,21 @@
     return attention.transpose(1, 0, 2).reshape(rows, head_count * HD)
 
 
-def gather_plane(rows):
+def plane_experts(rows, expert_of):
     near = [plane_shift(rows, by, 0) for by in (1, -1, 2)]
     rows = jnp.concatenate([rows] + near)
     half = rows.shape[0] // 2
     left, right = plane_shift(rows, 1, 1), plane_shift(rows, -1, 1)
     far_first = plane_shift(left[:half], 1, 1)
     far_second = plane_shift(right[half:], -1, 1)
-    mine = [rows, left, right, far_first, far_second]
-    return mine, [swap(block, "core") for block in mine]
+    mine = [rows, left, right]
+    other = [swap(block, "core") for block in mine]
+    near = expert_of(mine)
+    far_first, far_second, first = lax.optimization_barrier((far_first, far_second, near[0]))
+    other = expert_of(other + [swap(far_first, "core"), swap(far_second, "core")])
+    far_first, last = lax.optimization_barrier((far_first, other[4]))
+    far = expert_of([far_first, far_second])
+    return [first, *near[1:], *far], [*other[:4], last]
 
 
 def scatter_plane(mine, other):
@@ -178,7 +184,7 @@
         out_specs=[pl.BlockSpec((b.shape[0], wide), lambda i: (0, trail(i))) for b in blocks],
         out_shape=[jax.ShapeDtypeStruct(b.shape, BF) for b in blocks],
         scratch_shapes=[pltpu.VMEM((rows, 2 * units), F32), pltpu.VMEM((rows, units), BF)],
-        compiler_params=pltpu.CompilerParams(vmem_limit_bytes=40 * 1024 * 1024),
+        compiler_params=pltpu.CompilerParams(vmem_limit_bytes=30 * 1024 * 1024),
         cost_estimate=pl.CostEstimate(
             flops=6 * rows * features * units,
             bytes_accessed=2 * (3 * features * units + 2 * rows * features),
@@ -231,9 +237,9 @@
     incoming = lax.all_to_all(
         outgoing.reshape(EXPERTS, SLOTS, width), "z", split_axis=0, concat_axis=0, tiled=True
     ).reshape(EXPERTS * SLOTS, width)
-    mine, other = gather_plane(incoming)
     weights = w_gate[0], w_up[0], w_down[0]
-    slot_sums = scatter_plane(expert(mine, *weights), expert(other, *weights))
+    mine, other = plane_experts(incoming, lambda blocks: expert(blocks, *weights))
+    slot_sums = scatter_plane(mine, other)
     logits = jnp.dot(normed, w_router, preferred_element_type=F32)
     chosen = jnp.sum((routes[..., None] == expert_ids).astype(F32) * logits[:, None, :], axis=-1)
     gates = jax.nn.softmax(chosen, axis=-1)

time: 258 us -> 256 us (level)
  waiting for transfers between devices: 99.1 us -> 90.5 us
  local copies, waits for them, and re-layouts: 4.52 us -> 11 us
    ppermute x14, waiting for transfers between devices: 62.3 us -> 55.3 us  [plane_shift(): return lax.ppermute(value, PLANE, pairs)]
    unnamed x19 -> x31, local copies, waits for them, and re-layouts: 1.97 us -> 4.87 us
    pallas_call x2 -> x3, Pallas kernels: 15 us -> 13.3 us  [expert(): pl.pallas_call(functools.partial(expert_kernel, len(blocks)), grid=(2 * S...]
  transfers between devices with their start and end apart: 30 -> 30, of which waited for: 19 -> 18; matrix products, arithmetic and copies ran while one was open for 5% -> 5% of each run, Pallas kernels for 3% -> 3%
where the time goes in v3:
time: 256 us; the launch traced here: 255 us
  waiting for transfers between devices  90.5 us (35%)
  blocking collectives  82.5 us (32%)
  starting transfers between devices  26.8 us (10%)
  between operations  13.8 us (5%)
  Pallas kernels  13.3 us (5%)
  local copies, waits for them, and re-layouts  11 us (4%)
  other arithmetic  8.55 us (3%)
  matrix products  8.53 us (3%)
    ppermute x14, waiting for transfers between devices, plane_shift(): return lax.ppermute(value, PLANE, pairs)  55.3 us
    all_to_all x1, blocking collectives, shards(): lax.all_to_all(head_partial.reshape(16, tokens, width), EXP, split_axis=0...  48.6 us
    all_gather x1, waiting for transfers between devices, shards(): w_out_all = lax.all_gather(w_out, CTX, axis=1, tiled=True)  20.8 us
    all_to_all x1, blocking collectives, shards(): lax.all_to_all(outgoing.reshape(EXPERTS, SLOTS, width), 'z', split_axis=0...  19.1 us
    ppermute x14, starting transfers between devices, plane_shift(): return lax.ppermute(value, PLANE, pairs)  17.8 us
    all_to_all x1, blocking collectives, shards(): lax.all_to_all(slot_sums.reshape(EXPERTS, SLOTS, width), 'z', split_axis=...  14.8 us
    pallas_call x3, Pallas kernels, expert(): pl.pallas_call(functools.partial(expert_kernel, len(blocks)), grid=(2 * S...  13.3 us
    ppermute x12, waiting for transfers between devices, swap(): return lax.ppermute(value, axis, [(0, 1), (1, 0)])  10.8 us
  transfers between devices with their start and end apart: 30, of which 18 were waited for; matrix products, arithmetic and copies ran while one was open for 5% of the time, Pallas kernels for 3%

profile of v3, /device:TPU:32, one launch (start us, length us, event | category | flops | bytes accessed | tf_op | source)
XLA Modules:
  0.0 255.0 jit_solution(11506734682041166986)
XLA Ops:
  6.5 0.7 all-gather.2.cloned.1.call-update
  7.3 0.8 constant_dynamic-slice_fusion
  8.1 0.7 convert_bitcast_fusion
  8.7 2.8 %collective-permute-start.1 = (bf16[136,256]{1,0:T(8,128)(2,1)S(1)}, bf16[136,256]{1,0:T(8,128)(2,1)S(1)}, u32[]{:S(2)}, u32[]{:S(2)}) collective-permute-start(bf16[136,256]{1,0:T(8,128)(2,1)S(1)} %get-tuple-element.63), channel_id=1, source_target_pairs={{0,192},{64,0},{128,64},{192,128},{1,193},{65,1},{129,65},{193,129... | collective-permute-start | bytes 208904 | tf_op jit(solution)/shard_map/ppermute | solution.py:68
  11.6 2.3 collective-permute-start.2
  13.9 0.8 copy.30
  15.1 2.9 %collective-permute-done = bf16[136,256]{1,0:T(8,128)(2,1)S(1)} collective-permute-done((bf16[136,256]{1,0:T(8,128)(2,1)S(1)}, bf16[136,256]{1,0:T(8,128)(2,1)S(1)}, u32[]{:S(2)}, u32[]{:S(2)}) %collective-permute-start) | collective-permute-done | bytes 69664 | tf_op jit(solution)/shard_map/ppermute | solution.py:68
  18.0 1.7 collective-permute-start.3
  20.1 5.3 %collective-permute-done.3 = bf16[4,136,256]{2,1,0:T(8,128)(2,1)S(1)} collective-permute-done((bf16[4,136,256]{2,1,0:T(8,128)(2,1)S(1)}, bf16[4,136,256]{2,1,0:T(8,128)(2,1)S(1)}, u32[]{:S(2)}, u32[]{:S(2)}) %collective-permute-start.3) | collective-permute-done | bytes 278560 | tf_op jit(solution)/shard_map/ppermute | solution.py:24
  25.6 1.8 collective-permute-done.4
  27.6 0.3 fusion.35
  27.9 0.3 copy-done.12
  28.2 1.3 compare_and_fusion
  29.5 1.6 fusion.36
  31.1 1.5 fusion.13
  32.6 20.8 %all-gather.2.cloned.1.call-done = bf16[384,6144]{1,0:T(8,128)(2,1)} async-done(((bf16[384,384]{1,0:T(8,128)(2,1)}), bf16[384,6144]{1,0:T(8,128)(2,1)}) %all-gather.2.cloned.1.call-update) | async-done | bytes 4718608 | tf_op jit(solution)/shard_map/all_gather | solution.py:211
  53.4 3.4 %convolution_convert_fusion = bf16[128,6144]{1,0:T(8,128)(2,1)S(1)} fusion(bf16[128,384]{0,1:T(8,128)(2,1)S(1)} %bitcast.95, bf16[384,6144]{1,0:T(8,128)(2,1)} %all-gather.2.cloned.1.call-done), kind=kOutput, calls=%fused_computation.1 | convolution fusion | flops 604766208 | bytes 6389760 | tf_op jit(solution)/shard_map/dot_general | solution.py:213
  56.8 48.6 %all_to_all.15 = bf16[16,8,6144]{2,1,0:T(8,128)(2,1)S(1)} all-to-all(bf16[16,8,6144]{2,1,0:T(8,128)(2,1)S(1)} %bitcast.87), channel_id=1, replica_groups=mesh['x'=4,'yl'=2,'core'=2,'z'=8,'yh'=2] {'z','yh'}, dimensions={0} | all-to-all | bytes 3145728 | tf_op jit(solution)/shard_map/all_to_all | solution.py:227
  105.6 0.7 copy-done.7
  106.5 1.0 convolution_convert_fusion.1
  107.5 2.0 reshape.310
  109.6 19.1 %all_to_all.16 = bf16[8,3,6144]{2,1,0:T(4,128)(2,1)} all-to-all(bf16[8,3,6144]{2,1,0:T(4,128)(2,1)} %reshape.310), channel_id=1, replica_groups=mesh['x'=4,'yl'=2,'core'=2,'z'=8,'yh'=2] {'z'}, dimensions={0} | all-to-all | bytes 589824 | tf_op jit(solution)/shard_map/all_to_all | solution.py:237
  128.7 2.0 reshape.311
  130.7 2.5 collective-permute-start.7
  133.2 1.7 collective-permute-start.6
  134.9 0.3 collective-permute-start.5
  135.2 1.0 constant_dynamic-update-slice_fusion.3
  136.2 7.0 %collective-permute-done.5 = bf16[24,6144]{1,0:T(8,128)(2,1)S(1)} collective-permute-done((bf16[24,6144]{1,0:T(8,128)(2,1)}, bf16[24,6144]{1,0:T(8,128)(2,1)S(1)}, u32[]{:S(2)}, u32[]{:S(2)}) %collective-permute-start.5) | collective-permute-done | bytes 294944 | tf_op jit(solution)/shard_map/ppermute | solution.py:40
  143.4 0.3 collective-permute-start.10
  143.6 2.0 collective-permute-start.8
  145.7 14.2 %collective-permute-done.10.refs_2_ = bf16[96,6144]{1,0:T(8,128)(2,1)S(1)} collective-permute-done((bf16[96,6144]{1,0:T(8,128)(2,1)S(1)}, bf16[96,6144]{1,0:T(8,128)(2,1)S(1)}, u32[]{:S(2)}, u32[]{:S(2)}) %collective-permute-start.10) | collective-permute-done | bytes 1179680 | tf_op jit(solution)/shard_map/ppermute | solution.py:40
  159.9 1.3 collective-permute-start.11
  161.2 0.9 collective-permute-start.9
  162.1 0.5 collective-permute-start.14
  162.6 1.9 copy-done.3
  164.5 4.4 %expert.3 = (bf16[96,6144]{1,0:T(8,128)(2,1)S(1)}, bf16[96,6144]{1,0:T(8,128)(2,1)S(1)}, bf16[96,6144]{1,0:T(8,128)(2,1)S(1)}) custom-call(bf16[96,6144]{1,0:T(8,128)(2,1)S(1)} %constant_dynamic-update-slice_fusion.refs_0_, bf16[96,6144]{1,0:T(8,128)(2,1)S(1)} %collective-permute-done.8.refs_1_, bf16[96,6144]{1,0:T(8,128)(2,1)S(1)} %collective-permute-done.10.refs_2_, ...), custom_call_target="tpu_custom_call" | custom-call | flops 2717908992 | bytes 16515072 | tf_op jit(solution)/shard_map/expert/pallas_call | solution.py:179
  169.0 0.9 collective-permute-done.11.refs_1_
  169.8 2.5 collective-permute-done.9.refs_0_
  172.4 0.5 collective-permute-start.16
  172.9 1.5 collective-permute-done.15.refs_3_
  174.4 0.8 collective-permute-done.16.refs_4_
  175.3 6.2 %expert.4 = (bf16[96,6144]{1,0:T(8,128)(2,1)}, bf16[96,6144]{1,0:T(8,128)(2,1)S(1)}, bf16[96,6144]{1,0:T(8,128)(2,1)S(1)}, bf16[48,6144]{1,0:T(8,128)(2,1)S(1)}, bf16[48,6144]{1,0:T(8,128)(2,1)S(1)}) custom-call(bf16[96,6144]{1,0:T(8,128)(2,1)S(1)} %collective-permute-done.12.refs_0_, bf16[96,6144]{1,0:T(8,128)(2,1)S(1)} %collective-permute-done.13.refs_1_, ...), custom_call_target="tpu_custom_call" | custom-call | flops 3623878656 | bytes 18874368 | tf_op jit(solution)/shard_map/expert/pallas_call | solution.py:179
  181.6 0.4 collective-permute-start.19
  182.2 0.4 collective-permute-start.18
  182.7 2.7 %expert.5 = (bf16[48,6144]{1,0:T(8,128)(2,1)S(1)}, bf16[48,6144]{1,0:T(8,128)(2,1)S(1)}) custom-call(bf16[48,6144]{1,0:T(8,128)(2,1)S(1)} %collective-permute-done.9.refs_0_, bf16[48,6144]{1,0:T(8,128)(2,1)S(1)} %collective-permute-done.11.refs_1_, bf16[6144,256]{1,0:T(8,128)(2,1)S(1)} %bitcast.80, bf16[6144,256]{1,0:T(8,128)(2,1)S(1)} %bitcast.83, ...), custom_call_target="tpu_custom_call" | custom-call | flops 905969664 | bytes 11796480 | tf_op jit(solution)/shard_map/expert/pallas_call | solution.py:179
  185.8 2.0 collective-permute-start.23
  187.8 0.3 convert_add_fusion.1
  188.1 1.4 collective-permute-done.22
  189.4 0.3 convert_add_fusion
  189.8 5.8 %collective-permute-done.21 = bf16[48,6144]{1,0:T(8,128)(2,1)S(1)} collective-permute-done((bf16[48,6144]{1,0:T(8,128)(2,1)S(1)}, bf16[48,6144]{1,0:T(8,128)(2,1)S(1)}, u32[]{:S(2)}, u32[]{:S(2)}) %collective-permute-start.21) | collective-permute-done | bytes 589856 | tf_op jit(solution)/shard_map/ppermute | solution.py:40
  195.8 1.1 collective-permute-done.23
  197.1 1.1 pad_maximum_fusion.1
  198.3 1.9 collective-permute-start.25
  200.6 13.9 %collective-permute-done.24 = bf16[96,6144]{1,0:T(8,128)(2,1)} collective-permute-done((bf16[96,6144]{1,0:T(8,128)(2,1)S(1)}, bf16[96,6144]{1,0:T(8,128)(2,1)}, u32[]{:S(2)}, u32[]{:S(2)}) %collective-permute-start.24) | collective-permute-done | bytes 1179680 | tf_op jit(solution)/shard_map/ppermute | solution.py:40
  214.5 1.6 collective-permute-done.25
  216.1 2.7 %add_convert_fusion = bf16[96,6144]{1,0:T(8,128)(2,1)S(1)} fusion(bf16[96,6144]{1,0:T(8,128)(2,1)} %collective-permute-done.25, bf16[96,6144]{1,0:T(8,128)(2,1)} %collective-permute-done.24, bf16[96,6144]{1,0:T(8,128)(2,1)} %collective-permute-done.17, bf16[96,6144]{1,0:T(8,128)(2,1)S(1)} %copy-done.6), kind=kLoop, calls=%fused_computation.9 | loop fusion | flops 4718592 | bytes 5898240 | tf_op jit(solution)/shard_map/convert_element_type | solution.py:129
  218.8 1.6 collective-permute-start.26
  220.5 2.3 collective-permute-start.28
  222.8 0.7 collective-permute-start.27
  223.6 2.1 collective-permute-done.26
  225.6 3.2 %collective-permute-done.28 = bf16[24,6144]{1,0:T(8,128)(2,1)S(1)} collective-permute-done((bf16[24,6144]{1,0:T(8,128)(2,1)S(1)}, bf16[24,6144]{1,0:T(8,128)(2,1)S(1)}, u32[]{:S(2)}, u32[]{:S(2)}) %collective-permute-start.28) | collective-permute-done | bytes 294944 | tf_op jit(solution)/shard_map/ppermute | solution.py:40
  228.8 3.1 %collective-permute-done.27 = bf16[24,6144]{1,0:T(8,128)(2,1)S(1)} collective-permute-done((bf16[24,6144]{1,0:T(8,128)(2,1)S(1)}, bf16[24,6144]{1,0:T(8,128)(2,1)S(1)}, u32[]{:S(2)}, u32[]{:S(2)}) %collective-permute-start.27) | collective-permute-done | bytes 294944 | tf_op jit(solution)/shard_map/ppermute | solution.py:40
  232.2 14.8 %all_to_all.17 = bf16[8,3,6144]{2,1,0:T(4,128)(2,1)S(1)} all-to-all(bf16[8,3,6144]{2,1,0:T(4,128)(2,1)S(1)} %reshape.312), channel_id=1, replica_groups=mesh['x'=4,'yl'=2,'core'=2,'z'=8,'yh'=2] {'z'}, dimensions={0} | all-to-all | bytes 589824 | tf_op jit(solution)/shard_map/all_to_all | solution.py:248
  247.3 0.9 fusion.1
  (91 shorter events, 4.5 us)
Async XLA Ops:
  6.5 193.7 %copy-start = (bf16[6144,8]{0,1:T(8,128)(2,1)S(1)}, bf16[6144,8]{0,1:T(8,128)(2,1)}, u32[]{:S(2)}) copy-start(bf16[6144,8]{0,1:T(8,128)(2,1)} %param.19) | copy-start | bytes 294916
  6.5 13.3 %copy-start.9 = (bf16[128,384]{1,0:T(8,128)(2,1)S(1)}, bf16[128,384]{1,0:T(8,128)(2,1)}, u32[]{:S(2)}) copy-start(bf16[128,384]{1,0:T(8,128)(2,1)} %param.12) | copy-start | bytes 294916
  6.5 46.9 %all-gather.2.cloned.1.call-start = ((), (), s32[]{:S(2)}) async-start(), calls=%async_computation.3 | async-start | bytes 5013504 | tf_op jit(solution)/shard_map/all_gather | solution.py:211
  8.7 6.3 %collective-permute-start.1 = (bf16[136,256]{1,0:T(8,128)(2,1)S(1)}, bf16[136,256]{1,0:T(8,128)(2,1)S(1)}, u32[]{:S(2)}, u32[]{:S(2)}) collective-permute-start(bf16[136,256]{1,0:T(8,128)(2,1)S(1)} %get-tuple-element.63), channel_id=1, source_target_pairs={{0,192},{64,0},{128,64},{192,128},{1,193},{65,1},{129,65},{193,129... | collective-permute-start | bytes 208904 | tf_op jit(solution)/shard_map/ppermute | solution.py:68
  11.6 6.4 %collective-permute-start = (bf16[136,256]{1,0:T(8,128)(2,1)S(1)}, bf16[136,256]{1,0:T(8,128)(2,1)S(1)}, u32[]{:S(2)}, u32[]{:S(2)}) collective-permute-start(bf16[136,256]{1,0:T(8,128)(2,1)S(1)} %get-tuple-element.63), channel_id=1, source_target_pairs={{0,64},{64,128},{128,192},{192,0},{1,65},{65,129},{129,193},{193,1... | collective-permute-start | bytes 208904 | tf_op jit(solution)/shard_map/ppermute | solution.py:68
  11.6 6.4 %collective-permute-start.2 = (bf16[136,256]{1,0:T(8,128)(2,1)S(1)}, bf16[136,256]{1,0:T(8,128)(2,1)S(1)}, u32[]{:S(2)}, u32[]{:S(2)}) collective-permute-start(bf16[136,256]{1,0:T(8,128)(2,1)S(1)} %get-tuple-element.63), channel_id=1, source_target_pairs={{0,128},{64,192},{128,0},{192,64},{1,129},{65,193},{129,1},{193,65... | collective-permute-start | bytes 208904 | tf_op jit(solution)/shard_map/ppermute | solution.py:68
  18.0 7.3 %collective-permute-start.3 = (bf16[4,136,256]{2,1,0:T(8,128)(2,1)S(1)}, bf16[4,136,256]{2,1,0:T(8,128)(2,1)S(1)}, u32[]{:S(2)}, u32[]{:S(2)}) collective-permute-start(bf16[4,136,256]{2,1,0:T(8,128)(2,1)S(1)} %get-tuple-element.61), channel_id=1, source_target_pairs={{0,32},{32,0},{1,33},{33,1},{2,34},{34,2},{3,35},{35,3},{4,36},{36... | collective-permute-start | bytes 835592 | tf_op jit(solution)/shard_map/ppermute | solution.py:24
  25.4 2.0 collective-permute-start.4
  27.6 0.7 copy-start.12
  105.4 0.9 copy-start.7
  105.4 1.1 copy-start.10
  107.5 55.1 %copy-start.2 = (bf16[1,6144,256]{2,1,0:T(8,128)(2,1)S(1)}, bf16[1,6144,256]{2,1,0:T(8,128)(2,1)}, u32[]{:S(2)}) copy-start(bf16[1,6144,256]{2,1,0:T(8,128)(2,1)} %param.22) | copy-start | bytes 9437188
  130.7 12.7 %collective-permute-start.7 = (bf16[24,6144]{1,0:T(8,128)(2,1)}, bf16[24,6144]{1,0:T(8,128)(2,1)S(1)}, u32[]{:S(2)}, u32[]{:S(2)}) collective-permute-start(bf16[24,6144]{1,0:T(8,128)(2,1)} %reshape.311), channel_id=1, source_target_pairs={{0,128},{16,17},{32,160},{48,49},{1,129},{17,16},{33,161},{49,48},... | collective-permute-start | bytes 884744 | tf_op jit(solution)/shard_map/ppermute | solution.py:40
  133.2 10.1 %collective-permute-start.6 = (bf16[24,6144]{1,0:T(8,128)(2,1)}, bf16[24,6144]{1,0:T(8,128)(2,1)S(1)}, u32[]{:S(2)}, u32[]{:S(2)}) collective-permute-start(bf16[24,6144]{1,0:T(8,128)(2,1)} %reshape.311), channel_id=1, source_target_pairs={{0,192},{16,49},{32,224},{48,16},{1,193},{17,48},{33,225},{49,17},... | collective-permute-start | bytes 884744 | tf_op jit(solution)/shard_map/ppermute | solution.py:40
  134.9 8.4 %collective-permute-start.5 = (bf16[24,6144]{1,0:T(8,128)(2,1)}, bf16[24,6144]{1,0:T(8,128)(2,1)S(1)}, u32[]{:S(2)}, u32[]{:S(2)}) collective-permute-start(bf16[24,6144]{1,0:T(8,128)(2,1)} %reshape.311), channel_id=1, source_target_pairs={{0,64},{16,48},{32,96},{48,17},{1,65},{17,49},{33,97},{49,16},{64,... | collective-permute-start | bytes 884744 | tf_op jit(solution)/shard_map/ppermute | solution.py:40
  143.3 19.3 %copy-start.1 = (bf16[1,6144,256]{2,1,0:T(8,128)(2,1)S(1)}, bf16[1,6144,256]{2,1,0:T(8,128)(2,1)}, u32[]{:S(2)}) copy-start(bf16[1,6144,256]{2,1,0:T(8,128)(2,1)} %param.21) | copy-start | bytes 9437188
  143.4 16.5 %collective-permute-start.10 = (bf16[96,6144]{1,0:T(8,128)(2,1)S(1)}, bf16[96,6144]{1,0:T(8,128)(2,1)S(1)}, u32[]{:S(2)}, u32[]{:S(2)}) collective-permute-start(bf16[96,6144]{1,0:T(8,128)(2,1)S(1)} %constant_dynamic-update-slice_fusion.refs_0_), channel_id=1, source_target_pairs={{0,33},{16,208},{32,0},{48,240},{1,32},{17,209},{33,1},{49,241},{6... | collective-permute-start | bytes 3538952 | tf_op jit(solution)/shard_map/ppermute | solution.py:40
  143.6 17.5 %collective-permute-start.8 = (bf16[96,6144]{1,0:T(8,128)(2,1)S(1)}, bf16[96,6144]{1,0:T(8,128)(2,1)S(1)}, u32[]{:S(2)}, u32[]{:S(2)}) collective-permute-start(bf16[96,6144]{1,0:T(8,128)(2,1)S(1)} %constant_dynamic-update-slice_fusion.refs_0_), channel_id=1, source_target_pairs={{0,32},{16,80},{32,1},{48,112},{1,33},{17,81},{33,0},{49,113},{64,... | collective-permute-start | bytes 3538952 | tf_op jit(solution)/shard_map/ppermute | solution.py:40
  159.9 10.0 %collective-permute-start.11 = (bf16[48,6144]{1,0:T(8,128)(2,1)S(1)}, bf16[48,6144]{1,0:T(8,128)(2,1)S(1)}, u32[]{:S(2)}, u32[]{:S(2)}) collective-permute-start(bf16[48,6144]{1,0:T(8,128)(2,1)S(1)} %slice.62), channel_id=1, source_target_pairs={{0,33},{16,208},{32,0},{48,240},{1,32},{17,209},{33,1},{49,241},{6... | collective-permute-start | bytes 1769480 | tf_op jit(solution)/shard_map/ppermute | solution.py:40
  161.2 11.2 %collective-permute-start.9 = (bf16[48,6144]{1,0:T(8,128)(2,1)S(1)}, bf16[48,6144]{1,0:T(8,128)(2,1)S(1)}, u32[]{:S(2)}, u32[]{:S(2)}) collective-permute-start(bf16[48,6144]{1,0:T(8,128)(2,1)S(1)} %slice.61), channel_id=1, source_target_pairs={{0,32},{16,80},{32,1},{48,112},{1,33},{17,81},{33,0},{49,113},{64,... | collective-permute-start | bytes 1769480 | tf_op jit(solution)/shard_map/ppermute | solution.py:40
  162.1 10.8 %collective-permute-start.12 = (bf16[96,6144]{1,0:T(8,128)(2,1)S(1)}, bf16[96,6144]{1,0:T(8,128)(2,1)S(1)}, u32[]{:S(2)}, u32[]{:S(2)}) collective-permute-start(bf16[96,6144]{1,0:T(8,128)(2,1)S(1)} %constant_dynamic-update-slice_fusion.refs_0_), channel_id=1, source_target_pairs={{0,16},{16,0},{1,17},{17,1},{2,18},{18,2},{3,19},{19,3},{4,20},{20... | collective-permute-start | bytes 3538952 | tf_op jit(solution)/shard_map/ppermute | solution.py:24
  162.1 13.1 %collective-permute-start.14 = (bf16[96,6144]{1,0:T(8,128)(2,1)S(1)}, bf16[96,6144]{1,0:T(8,128)(2,1)S(1)}, u32[]{:S(2)}, u32[]{:S(2)}) collective-permute-start(bf16[96,6144]{1,0:T(8,128)(2,1)S(1)} %collective-permute-done.10.refs_2_), channel_id=1, source_target_pairs={{0,16},{16,0},{1,17},{17,1},{2,18},{18,2},{3,19},{19,3},{4,20},{20... | collective-permute-start | bytes 3538952 | tf_op jit(solution)/shard_map/ppermute | solution.py:24
  162.6 12.6 %collective-permute-start.13 = (bf16[96,6144]{1,0:T(8,128)(2,1)S(1)}, bf16[96,6144]{1,0:T(8,128)(2,1)S(1)}, u32[]{:S(2)}, u32[]{:S(2)}) collective-permute-start(bf16[96,6144]{1,0:T(8,128)(2,1)S(1)} %collective-permute-done.8.refs_1_), channel_id=1, source_target_pairs={{0,16},{16,0},{1,17},{17,1},{2,18},{18,2},{3,19},{19,3},{4,20},{20... | collective-permute-start | bytes 3538952 | tf_op jit(solution)/shard_map/ppermute | solution.py:24
  162.6 1.9 copy-start.3
  164.5 10.7 %copy-start.4 = (bf16[1,256,6144]{2,1,0:T(8,128)(2,1)S(1)}, bf16[1,256,6144]{2,1,0:T(8,128)(2,1)}, u32[]{:S(2)}) copy-start(bf16[1,256,6144]{2,1,0:T(8,128)(2,1)} %param.23) | copy-start | bytes 9437188
  169.0 12.6 %copy-start.5 = (bf16[96,6144]{1,0:T(8,128)(2,1)}, bf16[96,6144]{1,0:T(8,128)(2,1)S(1)}, u32[]{:S(2)}) copy-start(bf16[96,6144]{1,0:T(8,128)(2,1)S(1)} %get-tuple-element.32) | copy-start | bytes 3538948
  172.4 2.0 collective-permute-start.15
  172.4 2.8 %collective-permute-start.16 = (bf16[48,6144]{1,0:T(8,128)(2,1)S(1)}, bf16[48,6144]{1,0:T(8,128)(2,1)S(1)}, u32[]{:S(2)}, u32[]{:S(2)}) collective-permute-start(bf16[48,6144]{1,0:T(8,128)(2,1)S(1)} %collective-permute-done.11.refs_1_), channel_id=1, source_target_pairs={{0,16},{16,0},{1,17},{17,1},{2,18},{18,2},{3,19},{19,3},{4,20},{20... | collective-permute-start | bytes 1769480 | tf_op jit(solution)/shard_map/ppermute | solution.py:24
  181.5 3.8 %collective-permute-start.20 = (bf16[48,6144]{1,0:T(8,128)(2,1)S(1)}, bf16[48,6144]{1,0:T(8,128)(2,1)S(1)}, u32[]{:S(2)}, u32[]{:S(2)}) collective-permute-start(bf16[48,6144]{1,0:T(8,128)(2,1)S(1)} %get-tuple-element.43), channel_id=1, source_target_pairs={{0,16},{16,0},{1,17},{17,1},{2,18},{18,2},{3,19},{19,3},{4,20},{20... | collective-permute-start | bytes 1769480 | tf_op jit(solution)/shard_map/ppermute | solution.py:24
  181.6 3.9 %collective-permute-start.19 = (bf16[48,6144]{1,0:T(8,128)(2,1)S(1)}, bf16[48,6144]{1,0:T(8,128)(2,1)S(1)}, u32[]{:S(2)}, u32[]{:S(2)}) collective-permute-start(bf16[48,6144]{1,0:T(8,128)(2,1)S(1)} %get-tuple-element.41), channel_id=1, source_target_pairs={{0,16},{16,0},{1,17},{17,1},{2,18},{18,2},{3,19},{19,3},{4,20},{20... | collective-permute-start | bytes 1769480 | tf_op jit(solution)/shard_map/ppermute | solution.py:24
  182.0 18.6 %collective-permute-start.17 = (bf16[96,6144]{1,0:T(8,128)(2,1)}, bf16[96,6144]{1,0:T(8,128)(2,1)}, u32[]{:S(2)}, u32[]{:S(2)}) collective-permute-start(bf16[96,6144]{1,0:T(8,128)(2,1)} %get-tuple-element.35), channel_id=1, source_target_pairs={{0,16},{16,0},{1,17},{17,1},{2,18},{18,2},{3,19},{19,3},{4,20},{20... | collective-permute-start | bytes 3538952 | tf_op jit(solution)/shard_map/ppermute | solution.py:24
  182.2 5.6 %collective-permute-start.18 = (bf16[96,6144]{1,0:T(8,128)(2,1)S(1)}, bf16[96,6144]{1,0:T(8,128)(2,1)S(1)}, u32[]{:S(2)}, u32[]{:S(2)}) collective-permute-start(bf16[96,6144]{1,0:T(8,128)(2,1)S(1)} %get-tuple-element.37), channel_id=1, source_target_pairs={{0,16},{16,0},{1,17},{17,1},{2,18},{18,2},{3,19},{19,3},{4,20},{20... | collective-permute-start | bytes 3538952 | tf_op jit(solution)/shard_map/ppermute | solution.py:24
  182.5 6.9 %collective-permute-start.22 = (bf16[96,6144]{1,0:T(8,128)(2,1)S(1)}, bf16[96,6144]{1,0:T(8,128)(2,1)S(1)}, u32[]{:S(2)}, u32[]{:S(2)}) collective-permute-start(bf16[96,6144]{1,0:T(8,128)(2,1)S(1)} %get-tuple-element.46), channel_id=1, source_target_pairs={{0,16},{16,0},{1,17},{17,1},{2,18},{18,2},{3,19},{19,3},{4,20},{20... | collective-permute-start | bytes 3538952 | tf_op jit(solution)/shard_map/ppermute | solution.py:24
  185.7 10.0 %collective-permute-start.21 = (bf16[48,6144]{1,0:T(8,128)(2,1)S(1)}, bf16[48,6144]{1,0:T(8,128)(2,1)S(1)}, u32[]{:S(2)}, u32[]{:S(2)}) collective-permute-start(bf16[48,6144]{1,0:T(8,128)(2,1)S(1)} %add_convert_fusion.2), channel_id=1, source_target_pairs={{0,33},{16,208},{32,0},{48,240},{1,32},{17,209},{33,1},{49,241},{6... | collective-permute-start | bytes 1769480 | tf_op jit(solution)/shard_map/ppermute | solution.py:40
  185.8 11.2 %collective-permute-start.23 = (bf16[48,6144]{1,0:T(8,128)(2,1)S(1)}, bf16[48,6144]{1,0:T(8,128)(2,1)S(1)}, u32[]{:S(2)}, u32[]{:S(2)}) collective-permute-start(bf16[48,6144]{1,0:T(8,128)(2,1)S(1)} %add_convert_fusion.1), channel_id=1, source_target_pairs={{0,32},{16,80},{32,1},{48,112},{1,33},{17,81},{33,0},{49,113},{64,... | collective-permute-start | bytes 1769480 | tf_op jit(solution)/shard_map/ppermute | solution.py:40
  197.1 3.3 %copy-start.11 = (s32[8,2]{0,1:T(2,128)S(1)}, s32[8,2]{0,1:T(2,128)}, u32[]{:S(2)}) copy-start(s32[8,2]{0,1:T(2,128)} %param.20) | copy-start | bytes 196
  197.1 19.0 %copy-start.6 = (bf16[96,6144]{1,0:T(8,128)(2,1)S(1)}, bf16[96,6144]{1,0:T(8,128)(2,1)}, u32[]{:S(2)}) copy-start(bf16[96,6144]{1,0:T(8,128)(2,1)} %copy-done.5) | copy-start | bytes 3538948
  198.2 16.3 %collective-permute-start.24 = (bf16[96,6144]{1,0:T(8,128)(2,1)S(1)}, bf16[96,6144]{1,0:T(8,128)(2,1)}, u32[]{:S(2)}, u32[]{:S(2)}) collective-permute-start(bf16[96,6144]{1,0:T(8,128)(2,1)S(1)} %pad_maximum_fusion), channel_id=1, source_target_pairs={{0,33},{16,208},{32,0},{48,240},{1,32},{17,209},{33,1},{49,241},{6... | collective-permute-start | bytes 3538952 | tf_op jit(solution)/shard_map/ppermute | solution.py:40
  198.3 17.7 %collective-permute-start.25 = (bf16[96,6144]{1,0:T(8,128)(2,1)}, bf16[96,6144]{1,0:T(8,128)(2,1)}, u32[]{:S(2)}, u32[]{:S(2)}) collective-permute-start(bf16[96,6144]{1,0:T(8,128)(2,1)} %pad_maximum_fusion.1), channel_id=1, source_target_pairs={{0,32},{16,80},{32,1},{48,112},{1,33},{17,81},{33,0},{49,113},{64,... | collective-permute-start | bytes 3538952 | tf_op jit(solution)/shard_map/ppermute | solution.py:40
  218.8 6.8 %collective-permute-start.26 = (bf16[24,6144]{1,0:T(8,128)(2,1)S(1)}, bf16[24,6144]{1,0:T(8,128)(2,1)S(1)}, u32[]{:S(2)}, u32[]{:S(2)}) collective-permute-start(bf16[24,6144]{1,0:T(8,128)(2,1)S(1)} %get-tuple-element.53), channel_id=1, source_target_pairs={{0,192},{16,49},{32,224},{48,16},{1,193},{17,48},{33,225},{49,17},... | collective-permute-start | bytes 884744 | tf_op jit(solution)/shard_map/ppermute | solution.py:40
  220.5 8.3 %collective-permute-start.28 = (bf16[24,6144]{1,0:T(8,128)(2,1)S(1)}, bf16[24,6144]{1,0:T(8,128)(2,1)S(1)}, u32[]{:S(2)}, u32[]{:S(2)}) collective-permute-start(bf16[24,6144]{1,0:T(8,128)(2,1)S(1)} %get-tuple-element.54), channel_id=1, source_target_pairs={{0,128},{16,17},{32,160},{48,49},{1,129},{17,16},{33,161},{49,48},... | collective-permute-start | bytes 884744 | tf_op jit(solution)/shard_map/ppermute | solution.py:40
  222.8 9.1 %collective-permute-start.27 = (bf16[24,6144]{1,0:T(8,128)(2,1)S(1)}, bf16[24,6144]{1,0:T(8,128)(2,1)S(1)}, u32[]{:S(2)}, u32[]{:S(2)}) collective-permute-start(bf16[24,6144]{1,0:T(8,128)(2,1)S(1)} %get-tuple-element.55), channel_id=1, source_target_pairs={{0,64},{16,48},{32,96},{48,17},{1,65},{17,49},{33,97},{49,16},{64,... | collective-permute-start | bytes 884744 | tf_op jit(solution)/shard_map/ppermute | solution.py:40
  232.0 15.2 %copy-start.8 = (bf16[8,6144]{1,0:T(8,128)(2,1)S(1)}, bf16[8,6144]{1,0:T(8,128)(2,1)}, u32[]{:S(2)}) copy-start(bf16[8,6144]{1,0:T(8,128)(2,1)} %param.16) | copy-start | bytes 294916
Sparse Core Ops, SparseCore 0:
  9.2 44.1 all-gather.1
